TPU v7x, 256 devices: a whole 4x4x8 slice. The times are simulated.
256 devices in a mesh: row: 8 (over y, core), col: 32 (over x, z).
Axes of the slice: x: 4, y: 4, z: 8, core: 2. Of those that a mesh axis runs over, the one named last changes fastest.
Arguments:
- features: bfloat16 [262144, 256], P(('row', 'col')), may hold values from -12 to 12
- grad_out: bfloat16 [262144, 256], P(('row', 'col')), may hold values from -12 to 12
- conv_weight: bfloat16 [27, 256, 256], replicated, may hold values from -0.078125 to 0.078125
- pool_gain: float32 [5, 256], replicated, may hold values from -4 to 4
- neighbours: int32 [27, 262144], P(None, ('row', 'col')), may hold values from 0 to 1536, as said below
- requests: int32 [8192, 16], P(('row', 'col')), may hold values from 0 to 1023, as said below
- pool_mask: int32 [5, 262144], P(None, ('row', 'col')), may hold values 0 or 1
Outputs:
- feature_grad: bfloat16 [262144, 256], P(('row', 'col'))
- weight_grad: float32 [27, 256, 256], replicated
- gain_grad: float32 [5, 256], replicated
Inputs may be any that keep to these rules, and one draw needn't show every extreme that they name: `neighbours`: entry 13 of an octant is the octant itself. Toward each peer p of its row a device uses a prefix of its 16 ghost slots p * 16 .. p * 16 + n - 1: none toward itself, all 16 toward at least one peer, and every used slot is named by some octant. `requests`: unused slots also hold valid octant numbers of the peer.
All inputs are finite; a program needn't handle non-finite values. No bound on the sum of `pool_mask` on one device may be relied on, other than what follows from the above.
Results may differ from a plain program's by a relative error of at most 0.0045.
Values may be sent and summed in bfloat16 or wider, within the bound.
A program may use at most 128 MiB of HBM per device.

v0:
```python
import jax
import jax.numpy as jnp
from jax import lax
from jax.sharding import PartitionSpec as P

clip_norm = 1024.0
tiny_eps = 1e-06


def from_partner(value, axis, stride):
    mask = 2**stride
    pairs = [(source, source ^ mask) for source in range(lax.axis_size(axis))]
    return lax.ppermute(value, axis, pairs)


def on_device(features, grad_out, conv_weight, pool_gain, neighbours, requests, pool_mask):
    rows_here = features.shape[0]
    channels = features.shape[1]
    wanted = lax.all_to_all(requests, "col", split_axis=0, concat_axis=0, tiled=True)
    outgoing = features[wanted]
    ghosts = lax.all_to_all(outgoing, "col", split_axis=0, concat_axis=0, tiled=True)
    ghost_count = wanted.shape[0] * wanted.shape[1]
    extended = jnp.concatenate(
        [features, ghosts.reshape(ghost_count, channels), jnp.zeros((1, channels), jnp.bfloat16)],
        axis=0,
    )

    def one_tap(grad_rows, inputs):
        tap_index, tap_weight = inputs
        gathered = extended[tap_index]
        tap_grad = lax.dot_general(
            gathered, grad_out, (((0,), (0,)), ((), ())), preferred_element_type=jnp.float32
        )
        spread = lax.dot_general(
            grad_out, tap_weight, (((1,), (1,)), ((), ())), preferred_element_type=jnp.float32
        )
        return (grad_rows.at[tap_index].add(spread), tap_grad)

    grad_rows, weight_local = lax.scan(
        one_tap,
        jnp.zeros((rows_here + ghost_count + 1, channels), jnp.float32),
        (neighbours, conv_weight),
    )
    ghost_terms = grad_rows[rows_here : rows_here + ghost_count].reshape(
        wanted.shape[0], wanted.shape[1], channels
    )
    returned = lax.all_to_all(
        ghost_terms.astype(jnp.bfloat16), "col", split_axis=0, concat_axis=0, tiled=True
    ).astype(ghost_terms.dtype)
    conv_grad = (
        grad_rows[:rows_here].at[wanted.reshape(-1)].add(returned.reshape(ghost_count, channels))
    )
    mask_rows = pool_mask.astype(jnp.bfloat16)
    level_sums = jnp.dot(mask_rows, grad_out, preferred_element_type=jnp.float32)
    feature_sums = jnp.dot(mask_rows, features, preferred_element_type=jnp.float32)
    levels = pool_mask.shape[0]
    level_rows = jnp.arange(levels, dtype=jnp.int32)[:, None]
    col_count = lax.axis_size("col")
    row_count = lax.axis_size("row")
    col_bits = col_count.bit_length() - 1
    row_bits = row_count.bit_length() - 1
    total_bits = col_bits + row_bits
    summed = level_sums
    for level_index in range(levels):
        bit_number = total_bits - 1 - level_index
        if bit_number >= col_bits:
            partner = from_partner(summed, "row", bit_number - col_bits)
        else:
            partner = from_partner(summed, "col", bit_number)
        summed = summed + jnp.where(level_rows >= level_index, partner, 0.0)
    level_scale = jnp.array(
        [(2.0 ** (level_index + 1) * rows_here) ** (-0.5) for level_index in range(levels)],
        dtype=jnp.float32,
    )[:, None]
    pooled = summed * level_scale
    pool_term = jnp.dot(
        pool_mask.T.astype(jnp.float32), pooled * pool_gain, precision=lax.Precision.HIGHEST
    )
    feature_grad = (conv_grad + pool_term).astype(jnp.bfloat16)
    gain_term = feature_sums * pooled
    weight_total, gain_total = lax.psum((weight_local, gain_term), ("row", "col"))
    grad_norm = jnp.sqrt(
        jnp.sum(weight_total * weight_total) + jnp.sum(gain_total * gain_total) + tiny_eps
    )
    factor = jnp.minimum(1.0, clip_norm / grad_norm)
    return (feature_grad, weight_total * factor, gain_total * factor)


def solution(mesh):
    placed = (
        P(("row", "col"), None),
        P(("row", "col"), None),
        P(),
        P(),
        P(None, ("row", "col")),
        P(("row", "col"), None),
        P(None, ("row", "col")),
    )
    return jax.shard_map(
        on_device,
        mesh=mesh,
        in_specs=placed,
        out_specs=(P(("row", "col"), None), P(), P()),
        check_vma=False,
    )
```

profile of v0, /device:TPU:1, one launch (start us, length us, event | category | flops | bytes accessed | tf_op | source)
XLA Modules:
  0.0 781.6 jit_solution(2579115998152405491)
XLA Ops:
  8.0 20.3 %all_to_all.22 = s32[32,1,16]{2,1,0:T(1,128)S(1)} all-to-all(s32[32,1,16]{2,1,0:T(1,128)S(1)} %bitcast.53), channel_id=1, replica_groups=mesh['row'=8,'col'=32] {'col'}, dimensions={0} | all-to-all | bytes 4096 | tf_op jit(solution)/shard_map/all_to_all | solution.py:19
  35.7 9.6 %all-to-all-done.1 = bf16[32,16,256]{2,1,0:T(8,128)(2,1)S(1)} async-done(((bf16[32,16,256]{2,1,0:T(8,128)(2,1)}), bf16[32,16,256]{2,1,0:T(8,128)(2,1)S(1)}, u32[]{:S(2)}, u32[]{:S(2)}) %all-to-all-start.1) | async-done | bytes 262176 | tf_op jit(solution)/shard_map/all_to_all | solution.py:21
  46.7 437.2 %while.12 = (s32[]{:T(128)}, f32[1537,256]{1,0:T(8,128)S(1)}, f32[27,256,256]{2,1,0:T(8,128)}, s32[27,1024]{1,0:T(8,128)}, bf16[27,256,256]{2,1,0:T(8,128)(2,1)}...) while((s32[]{:T(128)}, f32[1537,256]{1,0:T(8,128)S(1)}, ...), condition=%wide.region_2.3_spmd, body=%wide.region_0.2_spmd.sunk | while | flops 268701696 | bytes 11427981 | solution.py:39
  51.3 6.6 scatter_fusion
  67.5 6.6 scatter_fusion
  83.7 6.6 scatter_fusion
  99.9 6.6 scatter_fusion
  116.1 6.6 scatter_fusion
  132.3 6.6 scatter_fusion
  148.5 6.6 scatter_fusion
  164.6 6.6 scatter_fusion
  180.8 6.6 scatter_fusion
  197.0 6.6 scatter_fusion
  213.2 6.6 scatter_fusion
  229.4 6.6 scatter_fusion
  245.6 6.6 scatter_fusion
  261.8 6.6 scatter_fusion
  278.0 6.6 scatter_fusion
  294.2 6.6 scatter_fusion
  310.4 6.6 scatter_fusion
  326.6 6.6 scatter_fusion
  342.8 6.6 scatter_fusion
  359.0 6.6 scatter_fusion
  375.2 6.6 scatter_fusion
  391.4 6.6 scatter_fusion
  407.6 6.6 scatter_fusion
  423.7 6.6 scatter_fusion
  439.9 6.6 scatter_fusion
  456.1 6.6 scatter_fusion
  508.6 78.6 %psum.15 = f32[5,256]{1,0:T(8,128)S(1)} all-reduce(f32[5,256]{1,0:T(8,128)S(1)} %convolution_multiply_fusion), channel_id=1, replica_groups=mesh['row'=8,'col'=32] {'row','col'}, use_global_device_ids=true, to_apply=%region_6.7 | all-reduce | flops 1280 | bytes 10240 | tf_op jit(solution)/shard_map/psum | solution.py:81
  597.0 163.7 %all-reduce.2.cloned.1.call-done = f32[27,256,256]{2,1,0:T(8,128)} async-done(((f32[27,256,256]{2,1,0:T(8,128)}), f32[27,256,256]{2,1,0:T(8,128)}) %all-reduce.2.cloned.1.call-update) | async-done | bytes 7077904 | tf_op jit(solution)/shard_map/psum | solution.py:81
  768.1 6.7 broadcast_multiply_fusion
  (274 shorter events, 314.5 us)
Async XLA Ops:
  7.2 39.5 %copy-start = (bf16[1024,256]{1,0:T(8,128)(2,1)S(1)}, bf16[1024,256]{1,0:T(8,128)(2,1)}, u32[]{:S(2)}) copy-start(bf16[1024,256]{1,0:T(8,128)(2,1)} %param.11) | copy-start | bytes 1572868
  31.7 13.6 %all-to-all-start.1 = ((bf16[32,16,256]{2,1,0:T(8,128)(2,1)}), bf16[32,16,256]{2,1,0:T(8,128)(2,1)S(1)}, u32[]{:S(2)}, u32[]{:S(2)}) async-start(bf16[32,16,256]{2,1,0:T(8,128)(2,1)} %bitcast.7), calls=%async_computation.1 | async-start | bytes 524288 | tf_op jit(solution)/shard_map/all_to_all | solution.py:21
  35.6 725.1 %all-reduce.2.cloned.1.call-start = ((), (), s32[]{:S(2)}) async-start(), calls=%async_computation.3 | async-start | bytes 14155776 | tf_op jit(solution)/shard_map/psum | solution.py:81
  57.9 4.0 copy-start.1
  90.3 4.0 copy-start.1
  106.5 4.0 copy-start.1
  122.7 4.0 copy-start.1
  138.9 4.0 copy-start.1
  155.0 4.0 copy-start.1
  171.2 4.0 copy-start.1
  187.4 4.0 copy-start.1
  203.6 4.0 copy-start.1
  219.8 4.0 copy-start.1
  236.0 4.0 copy-start.1
  268.4 4.0 copy-start.1
  300.8 4.0 copy-start.1
  317.0 4.0 copy-start.1
  333.2 4.0 copy-start.1
  349.4 4.0 copy-start.1
  365.6 4.0 copy-start.1
  381.8 4.0 copy-start.1
  414.1 4.0 copy-start.1
  446.5 4.0 copy-start.1
  484.0 24.4 %copy-start.2 = (bf16[1024,256]{1,0:T(8,128)(2,1)S(1)}, bf16[1024,256]{1,0:T(8,128)(2,1)}, u32[]{:S(2)}) copy-start(bf16[1024,256]{1,0:T(8,128)(2,1)} %param.10) | copy-start | bytes 1572868
  484.0 24.4 %copy-start.5 = (f32[5]{0:T(128)S(1)}, f32[5]{0:T(128)}, u32[]{:S(2)}) copy-start(f32[5]{0:T(128)} %constant.15.clone) | copy-start | bytes 64
  484.7 104.8 %copy-start.4 = (f32[5,256]{1,0:T(8,128)S(1)}, f32[5,256]{1,0:T(8,128)}, u32[]{:S(2)}) copy-start(f32[5,256]{1,0:T(8,128)} %param.13) | copy-start | bytes 15364
  484.9 4.0 collective-permute-start
  488.9 2.5 collective-permute-start.1
  491.5 6.8 collective-permute-start.2
  498.4 4.1 collective-permute-start.3
  502.5 5.9 collective-permute-start.4
  503.9 88.3 %all-to-all-start.2 = ((bf16[32,16,256]{2,1,0:T(8,128)(2,1)}), bf16[32,16,256]{2,1,0:T(8,128)(2,1)S(1)}, u32[]{:S(2)}, u32[]{:S(2)}) async-start(bf16[32,16,256]{2,1,0:T(8,128)(2,1)} %bitcast.11), calls=%async_computation.2 | async-start | bytes 524288 | tf_op jit(solution)/shard_map/all_to_all | solution.py:47
  (8 other events, 28.6 us)
Sparse Core Ops, SparseCore 0:
  484.1 276.5 all-reduce.1
where the time goes:
time: 786 us; the launch traced here: 782 us
  other arithmetic  219 us (28%)
  waiting for transfers between devices  178 us (23%)
  local copies, waits for them, and re-layouts  157 us (20%)
  blocking collectives  98.9 us (13%)
  matrix products  91.3 us (12%)
  starting transfers between devices  20.6 us (3%)
  between operations  15.5 us (2%)
    scatter-add x27, other arithmetic, one_tap(): return (grad_rows.at[tap_index].add(spread), tap_grad)  178 us
    psum x1, waiting for transfers between devices, on_device(): lax.psum((weight_local, gain_term), ('row', 'col'))  164 us
    gather x27, local copies, waits for them, and re-layouts, one_tap(): gathered = extended[tap_index]  106 us
    psum x1, blocking collectives, on_device(): lax.psum((weight_local, gain_term), ('row', 'col'))  78.6 us
    dot_general x27, matrix products, one_tap(): lax.dot_general(grad_out, tap_weight, (((1,), (1,)), ((), ())), preferred...  60.3 us
    dot_general x27, local copies, waits for them, and re-layouts, one_tap(): lax.dot_general(grad_out, tap_weight, (((1,), (1,)), ((), ())), preferred...  41.9 us
    dot_general x27, matrix products, one_tap(): lax.dot_general(gathered, grad_out, (((0,), (0,)), ((), ())), preferred_e...  28.3 us
    select_n x27, other arithmetic, one_tap(): return (grad_rows.at[tap_index].add(spread), tap_grad)  20.7 us
  transfers between devices with their start and end apart: 8, of which 6 were waited for; matrix products, arithmetic and copies ran while one was open for 2% of the time, Pallas kernels for 0%

commit v1 on v0

v1 whole, which is shorter than its diff:
```python
import jax
import jax.numpy as jnp
from jax import lax
from jax.experimental import pallas as pl
from jax.experimental.pallas import tpu as pltpu
from jax.sharding import PartitionSpec as P

MESH = pl.DeviceIdType.MESH
clip_norm = 1024.0
tiny_eps = 1e-06
ROWS = 1024
C = 256
TAPS = 27
BUCKET = 16
PEERS = 32
GHOSTS = PEERS * BUCKET
SLOTS = ROWS + GHOSTS
LEV = 5
T = 4
NG = 28 // T
R = T * C
HALF = R // 2
QUARTER = HALF // 4
PIECE = HALF // 16
AHEAD = 2
LAST_H = NG - AHEAD
STEPS = NG + 7
f32 = jnp.float32
bf16 = jnp.bfloat16


def wait_for(ref, sem):
    pltpu.make_async_copy(ref, ref, sem).wait()


def whole(
    features_ref,
    grad_ref,
    neighbours_ref,
    requests_ref,
    mask_ref,
    gain_ref,
    weight_hbm,
    fgrad_ref,
    wsum_ref,
    gain_out,
    scale_out,
    spread,
    ext_t,
    wpart,
    r0,
    a1,
    r1,
    a2,
    r2,
    r3,
    weight,
    total,
    wanted,
    owner_t,
    outgoing,
    ghosts,
    terms,
    returned,
    maskf,
    gainf,
    level_out,
    level_in,
    pooled,
    gains0,
    gains_y,
    gains_x,
    gains_z,
    squares,
    send,
    recv,
    halo_send,
    halo_recv,
    level_send,
    level_recv,
    gain_send,
    gain_recv,
    weight_sem,
):
    row = lax.axis_index("row")
    col = lax.axis_index("col")
    y = row // 2
    core = row % 2
    x = col // 8
    z = col % 8

    def push(src, dst, send_sem, recv_sem, device):
        pltpu.make_async_remote_copy(
            src_ref=src,
            dst_ref=dst,
            send_sem=send_sem,
            recv_sem=recv_sem,
            device_id=device,
            device_id_type=MESH,
        ).start()

    weight_copy = pltpu.make_async_copy(weight_hbm, weight, weight_sem)
    weight_copy.start()

    barrier = pltpu.get_barrier_semaphore()

    def greet(offset, carry):
        pl.semaphore_signal(
            barrier, inc=1, device_id=(row, (col + offset) % PEERS), device_id_type=MESH
        )
        return carry

    lax.fori_loop(1, PEERS, greet, 0)
    pl.semaphore_signal(barrier, inc=1, device_id=(y * 2 + 1 - core, col), device_id_type=MESH)
    for offset in range(1, 4):
        pl.semaphore_signal(
            barrier, inc=1, device_id=((y + offset) % 4 * 2 + core, col), device_id_type=MESH
        )

    maskf[...] = jnp.zeros_like(maskf)
    maskf[0:LEV, :] = mask_ref[...].astype(f32)
    gainf[...] = jnp.zeros_like(gainf)
    gainf[0:LEV, :] = gain_ref[...]
    level_out[0] = jnp.dot(maskf[...].astype(bf16), grad_ref[...], preferred_element_type=f32)
    wanted[pl.ds(col, 1)] = jnp.zeros((1, 1, 128), jnp.int32)
    own = pl.ds(pl.multiple_of(col * BUCKET, BUCKET), BUCKET)
    ghosts[own, :] = jnp.zeros((BUCKET, C), bf16)
    returned[own, :] = jnp.zeros((BUCKET, C), bf16)
    wpart[TAPS * C :, :] = jnp.zeros(((NG * T - TAPS) * C, C), f32)
    squares[...] = jnp.zeros_like(squares)
    total[...] = jnp.zeros_like(total)

    pl.semaphore_wait(barrier, PEERS - 1 + 1 + 3)

    def ask(offset, carry):
        peer = (col + offset) % PEERS
        push(requests_ref.at[peer], wanted.at[col], halo_send.at[0], halo_recv.at[0], (row, peer))
        return carry

    lax.fori_loop(1, PEERS, ask, 0)

    level_partner = (
        ((y + 2) % 4 * 2 + core, col),
        ((y + 1 - 2 * (y % 2)) * 2 + core, col),
        (y * 2 + 1 - core, col),
        (row, (x + 2) % 4 * 8 + z),
        (row, (x + 1 - 2 * (x % 2)) * 8 + z),
    )

    def level_start(level):
        push(
            level_out.at[level],
            level_in.at[level],
            level_send.at[level],
            level_recv.at[level],
            level_partner[level],
        )

    level_rows = lax.broadcasted_iota(jnp.int32, (8, C), 0)

    def level_end(level):
        wait_for(level_in.at[level], level_recv.at[level])
        summed = level_out[level] + jnp.where(level_rows >= level, level_in[level], 0.0)
        if level < LEV - 1:
            level_out[level + 1] = summed
            level_start(level + 1)
            return
        scale = jnp.zeros((8, C), f32)
        for row_level in range(LEV):
            value = (2.0 ** (row_level + 1) * ROWS) ** (-0.5)
            scale = jnp.where(level_rows == row_level, value, scale)
        pooled[...] = summed * scale
        feature_sums = jnp.dot(
            maskf[...].astype(bf16), features_ref[...], preferred_element_type=f32
        )
        gains0[0] = feature_sums * pooled[...]
        push(
            gains0.at[0], gains0.at[1], gain_send.at[0], gain_recv.at[0], (y * 2 + 1 - core, col)
        )

    def gain_stage(stage):
        if stage == 1:
            wait_for(gains0.at[1], gain_recv.at[0])
            gains_y[pl.ds(y, 1)] = (gains0[0] + gains0[1])[None]
            for offset in range(1, 4):
                device = ((y + offset) % 4 * 2 + core, col)
                push(gains_y.at[y], gains_y.at[y], gain_send.at[1], gain_recv.at[1], device)
        elif stage == 2:
            wait_for(gains_y.at[0:3], gain_recv.at[1])
            gains_x[pl.ds(x, 1)] = jnp.sum(gains_y[...], axis=0, keepdims=True)
            for offset in range(1, 4):
                device = (row, (x + offset) % 4 * 8 + z)
                push(gains_x.at[x], gains_x.at[x], gain_send.at[2], gain_recv.at[2], device)
        else:
            wait_for(gains_x.at[0:3], gain_recv.at[2])
            gains_z[pl.ds(z, 1)] = jnp.sum(gains_x[...], axis=0, keepdims=True)
            for offset in range(1, 8):
                device = (row, x * 8 + (z + offset) % 8)
                push(gains_z.at[z], gains_z.at[z], gain_send.at[3], gain_recv.at[3], device)

    level_start(0)

    ext_t[:, 0:ROWS] = features_ref[...].T

    def spread_taps(group):
        def one_tap(tap, carry):
            index = neighbours_ref[pl.ds(tap, 1), :]
            for first in range(0, SLOTS, 256):
                places = lax.broadcasted_iota(jnp.int16, (256, ROWS), 0)
                hit = places == (index - first).astype(jnp.int16)
                chosen = jnp.where(hit, bf16(1), bf16(0))
                part = jnp.dot(chosen, grad_ref[...], preferred_element_type=f32)
                spread[tap, first : first + 256, :] = part.astype(bf16)
            return carry

        lax.fori_loop(group * T, jnp.minimum(group * T + T, TAPS), one_tap, 0)

    def weight_taps(group):
        def one_tap(tap, carry):
            wpart[pl.ds(pl.multiple_of(tap * C, C), C), :] = jnp.dot(
                ext_t[...], spread[tap], preferred_element_type=f32
            )
            return carry

        lax.fori_loop(group * T, jnp.minimum(group * T + T, TAPS), one_tap, 0)

    def prologue(group, carry):
        spread_taps(group)

        @pl.when(group == 0)
        def _():
            wait_for(wanted.at[0 : PEERS - 1], halo_recv.at[0])
            lists = jnp.broadcast_to(wanted[...], (PEERS, BUCKET, 128)).reshape(GHOSTS, 128)
            lanes = lax.broadcasted_iota(jnp.int32, (GHOSTS, 128), 1)
            places = lax.broadcasted_iota(jnp.int32, (GHOSTS, 128), 0) % BUCKET
            picked = jnp.where(lanes == places, lists.astype(f32), 0.0)
            octant = jnp.sum(picked, axis=1, keepdims=True).astype(jnp.int32)
            octants = lax.broadcasted_iota(jnp.int32, (GHOSTS, ROWS), 1)
            chosen = jnp.where(octants == octant, 1.0, 0.0).astype(bf16)
            outgoing[...] = jnp.dot(chosen, features_ref[...], preferred_element_type=f32).astype(
                bf16
            )

            def give(offset, carry):
                peer = (col + offset) % PEERS
                there = pl.ds(pl.multiple_of(peer * BUCKET, BUCKET), BUCKET)
                push(
                    outgoing.at[there],
                    ghosts.at[own],
                    halo_send.at[1],
                    halo_recv.at[1],
                    (row, peer),
                )
                return carry

            lax.fori_loop(1, PEERS, give, 0)
            owner_t[...] = chosen.T

        return carry

    lax.fori_loop(0, AHEAD, prologue, 0)
    wait_for(ghosts.at[0 : GHOSTS - BUCKET], halo_recv.at[1])
    ext_t[:, ROWS:] = ghosts[...].T

    def first_of(group):
        odd = group % 2
        return odd, y + (x - y) * odd, x + (y - x) * odd

    def peer_first(odd, other):
        return ((other + (y - other) * odd) * 2 + core, (x + (other - x) * odd) * 8 + z)

    def peer_second(odd, other):
        return ((y + (other - y) * odd) * 2 + core, (other + (x - other) * odd) * 8 + z)

    other_core = (y * 2 + 1 - core, col)

    def rows_of(start, size):
        return pl.ds(pl.multiple_of(start, PIECE), size)

    def stage0(group):
        weight_taps(group)
        base = group * R
        push(
            wpart.at[rows_of(base + (1 - core) * HALF, HALF)],
            r0.at[group],
            send.at[0, group],
            recv.at[0, group],
            other_core,
        )

    def stage1(group):
        odd, first, second = first_of(group)
        wait_for(r0.at[group], recv.at[0, group])
        mine = rows_of(group * R + core * HALF, HALF)
        a1[group] = (wpart[mine, :] + r0[group]).astype(bf16)
        for offset in range(1, 4):
            other = (first + offset) % 4
            push(
                a1.at[group, rows_of(other * QUARTER, QUARTER)],
                r1.at[group, offset - 1],
                send.at[1, group],
                recv.at[1, group],
                peer_first(odd, other),
            )

    def stage2(group):
        odd, first, second = first_of(group)
        wait_for(r1.at[group], recv.at[1, group])
        mine = rows_of(group * R + core * HALF + first * QUARTER, QUARTER)
        kept = wpart[mine, :] + r0[group, rows_of(first * QUARTER, QUARTER), :]
        for offset in range(3):
            kept = kept + r1[group, offset].astype(f32)
        a2[group] = kept.astype(bf16)
        for offset in range(1, 4):
            other = (second + offset) % 4
            push(
                a2.at[group, rows_of(other * PIECE, PIECE)],
                r2.at[group, offset - 1],
                send.at[2, group],
                recv.at[2, group],
                peer_second(odd, other),
            )

    def stage3(group):
        odd, first, second = first_of(group)
        wait_for(r2.at[group], recv.at[2, group])
        kept = a2[group, rows_of(second * PIECE, PIECE), :].astype(f32)
        for offset in range(3):
            kept = kept + r2[group, offset].astype(f32)
        r3[group, pl.ds(z, 1)] = kept.astype(bf16)[None]
        for offset in range(1, 8):
            push(
                r3.at[group, z],
                r3.at[group, z],
                send.at[3, group],
                recv.at[3, group],
                (row, x * 8 + (z + offset) % 8),
            )

    def stage4(group):
        odd, first, second = first_of(group)
        wait_for(r3.at[group, 0:7], recv.at[3, group])
        kept = r3[group, 0].astype(f32)
        for place in range(1, 8):
            kept = kept + r3[group, place].astype(f32)
        mine = rows_of(group * R + core * HALF + first * QUARTER + second * PIECE, PIECE)
        wsum_ref[mine, :] = kept.astype(bf16)
        for offset in range(1, 4):
            other = (second + offset) % 4
            push(
                wsum_ref.at[mine],
                wsum_ref.at[mine],
                send.at[4, group],
                recv.at[4, group],
                peer_second(odd, other),
            )

    def stage5(group):
        odd, first, second = first_of(group)
        wait_for(r2.at[group], recv.at[4, group])
        mine = rows_of(group * R + core * HALF + first * QUARTER, QUARTER)
        for offset in range(1, 4):
            other = (first + offset) % 4
            push(
                wsum_ref.at[mine],
                wsum_ref.at[mine],
                send.at[5, group],
                recv.at[5, group],
                peer_first(odd, other),
            )

    def stage6(group):
        wait_for(r1.at[group], recv.at[5, group])
        mine = rows_of(group * R + core * HALF, HALF)
        push(
            wsum_ref.at[mine],
            wsum_ref.at[mine],
            send.at[6, group],
            recv.at[6, group],
            other_core,
        )

    def stage7(group):
        wait_for(a1.at[group], recv.at[6, group])

        def chunk(part, carry):
            value = wsum_ref[rows_of(group * R + part * 64, 64), :].astype(f32)
            squares[...] += jnp.sum((value * value).reshape(8, 8, C), axis=0)
            return carry

        lax.fori_loop(0, R // 64, chunk, 0)

    stages = (stage0, stage1, stage2, stage3, stage4, stage5, stage6, stage7)

    def conv_tap(tap, start, size):
        total[start : start + size, :] += lax.dot_general(
            spread[tap, start : start + size, :],
            weight[tap],
            (((1,), (1,)), ((), ())),
            preferred_element_type=f32,
        )

    def step(now, carry):
        for late, stage in enumerate(stages):
            group = now - late

            @pl.when(jnp.logical_and(group >= 0, group < NG))
            def _(stage=stage, group=group):
                stage(group)

        for level in range(LEV):

            @pl.when(now == level)
            def _(level=level):
                level_end(level)

        for stage in range(1, 4):

            @pl.when(now == LEV - 1 + stage)
            def _(stage=stage):
                gain_stage(stage)

        @pl.when(now < LAST_H)
        def _():
            spread_taps(now + AHEAD)

        @pl.when(now == LAST_H)
        def _():
            weight_copy.wait()

            def ghost_tap(tap, carry):
                conv_tap(tap, ROWS, GHOSTS)
                return carry

            lax.fori_loop(0, TAPS, ghost_tap, 0)
            terms[...] = total[ROWS:, :].astype(bf16)

            def give_back(offset, carry):
                peer = (col + offset) % PEERS
                there = pl.ds(pl.multiple_of(peer * BUCKET, BUCKET), BUCKET)
                push(
                    terms.at[there],
                    returned.at[own],
                    halo_send.at[2],
                    halo_recv.at[2],
                    (row, peer),
                )
                return carry

            lax.fori_loop(1, PEERS, give_back, 0)

        @pl.when(now > LAST_H)
        def _():
            def own_tap(tap, carry):
                conv_tap(tap, 0, ROWS)
                return carry

            begin = jnp.minimum((now - LAST_H - 1) * 5, TAPS)
            lax.fori_loop(begin, jnp.minimum(begin + 5, TAPS), own_tap, 0)

        @pl.when(now == LAST_H + 7)
        def _():
            wait_for(returned.at[0 : GHOSTS - BUCKET], halo_recv.at[2])
            term = pooled[...] * gainf[...]
            high = term.astype(bf16)
            rest = term - high.astype(f32)
            middle = rest.astype(bf16)
            low = (rest - middle.astype(f32)).astype(bf16)
            mask_rows = maskf[...]
            masks = jnp.concatenate([mask_rows, mask_rows, mask_rows], axis=0).T.astype(bf16)
            parts = jnp.concatenate([high.astype(f32), middle.astype(f32), low.astype(f32)], axis=0)
            for first in range(0, ROWS, 256):
                block = slice(first, first + 256)
                value = total[block, :] + jnp.dot(
                    owner_t[block, :], returned[...], preferred_element_type=f32
                )
                value = value + jnp.dot(
                    masks[block, :], parts.astype(bf16), preferred_element_type=f32
                )
                fgrad_ref[block, :] = value.astype(bf16)

        return carry

    lax.fori_loop(0, STEPS, step, 0)

    wait_for(gains_z.at[0:7], gain_recv.at[3])
    gain_total = gains_z[0]
    for place in range(1, 8):
        gain_total = gain_total + gains_z[place]
    both = squares[...] + gain_total * gain_total
    norm2 = jnp.sum(jnp.sum(both, axis=1, keepdims=True), axis=0, keepdims=True) + tiny_eps
    factor = jnp.minimum(1.0, clip_norm / jnp.sqrt(norm2))
    gain_out[...] = gain_total * factor
    scale_out[...] = jnp.broadcast_to(factor, (8, 128))

    def finish(group, carry):
        wait_for(r0.at[group], send.at[0, group])
        wait_for(r1.at[group], send.at[1, group])
        wait_for(r2.at[group], send.at[2, group])
        wait_for(r3.at[group, 0:7], send.at[3, group])
        wait_for(r2.at[group], send.at[4, group])
        wait_for(r1.at[group], send.at[5, group])
        wait_for(a1.at[group], send.at[6, group])
        return carry

    lax.fori_loop(0, NG, finish, 0)
    wait_for(wanted.at[0 : PEERS - 1], halo_send.at[0])
    wait_for(ghosts.at[0 : GHOSTS - BUCKET], halo_send.at[1])
    wait_for(ghosts.at[0 : GHOSTS - BUCKET], halo_send.at[2])
    for level in range(LEV):
        wait_for(level_in.at[level], level_send.at[level])
    wait_for(gains0.at[0], gain_send.at[0])
    wait_for(gains_y.at[0:3], gain_send.at[1])
    wait_for(gains_x.at[0:3], gain_send.at[2])
    wait_for(gains_z.at[0:7], gain_send.at[3])


def on_device(features, grad_out, conv_weight, pool_gain, neighbours, requests, pool_mask):
    lists = jnp.pad(requests, ((0, 0), (0, 128 - BUCKET)))[:, None, :]
    vmem = pl.BlockSpec(memory_space=pltpu.VMEM)
    dma = pltpu.SemaphoreType.DMA
    feature_grad, weight_sum, gain_grad, scale = pl.pallas_call(
        whole,
        out_shape=(
            jax.ShapeDtypeStruct((ROWS, C), bf16),
            jax.ShapeDtypeStruct((NG * R, C), bf16),
            jax.ShapeDtypeStruct((8, C), f32),
            jax.ShapeDtypeStruct((8, 128), f32),
        ),
        in_specs=[vmem] * 6 + [pl.BlockSpec(memory_space=pl.ANY)],
        out_specs=(vmem, vmem, vmem, vmem),
        scratch_shapes=[
            pltpu.VMEM((TAPS, SLOTS, C), bf16),
            pltpu.VMEM((C, SLOTS), bf16),
            pltpu.VMEM((NG * R, C), f32),
            pltpu.VMEM((NG, HALF, C), f32),
            pltpu.VMEM((NG, HALF, C), bf16),
            pltpu.VMEM((NG, 3, QUARTER, C), bf16),
            pltpu.VMEM((NG, QUARTER, C), bf16),
            pltpu.VMEM((NG, 3, PIECE, C), bf16),
            pltpu.VMEM((NG, 8, PIECE, C), bf16),
            pltpu.VMEM((TAPS, C, C), bf16),
            pltpu.VMEM((SLOTS, C), f32),
            pltpu.VMEM((PEERS, 1, 128), jnp.int32),
            pltpu.VMEM((ROWS, GHOSTS), bf16),
            pltpu.VMEM((GHOSTS, C), bf16),
            pltpu.VMEM((GHOSTS, C), bf16),
            pltpu.VMEM((GHOSTS, C), bf16),
            pltpu.VMEM((GHOSTS, C), bf16),
            pltpu.VMEM((8, ROWS), f32),
            pltpu.VMEM((8, C), f32),
            pltpu.VMEM((LEV, 8, C), f32),
            pltpu.VMEM((LEV, 8, C), f32),
            pltpu.VMEM((8, C), f32),
            pltpu.VMEM((2, 8, C), f32),
            pltpu.VMEM((4, 8, C), f32),
            pltpu.VMEM((4, 8, C), f32),
            pltpu.VMEM((8, 8, C), f32),
            pltpu.VMEM((8, C), f32),
            dma((7, NG)),
            dma((7, NG)),
            dma((3,)),
            dma((3,)),
            dma((LEV,)),
            dma((LEV,)),
            dma((4,)),
            dma((4,)),
            dma,
        ],
        compiler_params=pltpu.CompilerParams(
            collective_id=0, has_side_effects=True, vmem_limit_bytes=58 * 2**20
        ),
    )(features, grad_out, neighbours, lists, pool_mask, pool_gain, conv_weight)
    weight_sum = weight_sum[: TAPS * C].reshape(TAPS, C, C)
    return (feature_grad, weight_sum.astype(f32) * scale[0, 0], gain_grad[:LEV])


def solution(mesh):
    placed = (
        P(("row", "col"), None),
        P(("row", "col"), None),
        P(),
        P(),
        P(None, ("row", "col")),
        P(("row", "col"), None),
        P(None, ("row", "col")),
    )
    return jax.shard_map(
        on_device,
        mesh=mesh,
        in_specs=placed,
        out_specs=(P(("row", "col"), None), P(), P()),
        check_vma=False,
    )
```

time: 786 us -> 113 us (0.14)
  other arithmetic: 219 us -> 6.06 us
  waiting for transfers between devices: 178 us -> 0 us
  local copies, waits for them, and re-layouts: 157 us -> 4.02 us
  Pallas kernels: 0 us -> 102 us
  blocking collectives: 98.9 us -> 0 us
  matrix products: 91.3 us -> 0 us
  starting transfers between devices: 20.6 us -> 0 us
  between operations: 15.5 us -> 0.66 us
    scatter-add x28 -> x0, other arithmetic: 182 us -> none  [the longest x27 178 us: one_tap(): return (grad_rows.at[tap_index].add(spread), tap_grad)]
    psum x1 -> x0, waiting for transfers between devices: 164 us -> none  [on_device(): lax.psum((weight_local, gain_term), ('row', 'col'))]
    gather x28 -> x0, local copies, waits for them, and re-layouts: 110 us -> none  [the longest x27 106 us: one_tap(): gathered = extended[tap_index]]
    pallas_call x0 -> x1, Pallas kernels: none -> 102 us  [on_device(): pl.pallas_call(whole, out_shape=(jax.ShapeDtypeStruct((ROWS, C), bf16), j...]
    dot_general x57 -> x0, matrix products: 91.3 us -> none  [the longest x27 60.3 us: one_tap(): lax.dot_general(grad_out, tap_weight, (((1,), (1,)), ((), ())), preferred...]
    psum x1 -> x0, blocking collectives: 78.6 us -> none  [on_device(): lax.psum((weight_local, gain_term), ('row', 'col'))]
    dot_general x27 -> x0, local copies, waits for them, and re-layouts: 41.9 us -> none  [one_tap(): lax.dot_general(grad_out, tap_weight, (((1,), (1,)), ((), ())), preferred...]
    select_n x29 -> x0, other arithmetic: 20.7 us -> none  [the longest x27 20.7 us: one_tap(): return (grad_rows.at[tap_index].add(spread), tap_grad)]
  transfers between devices with their start and end apart: 8 -> 0, of which waited for: 6 -> 0; matrix products, arithmetic and copies ran while one was open for 2% -> 0% of each run, Pallas kernels for 0% -> 0%
where the time goes in v1:
time: 113 us
  Pallas kernels  102 us (90%)
  other arithmetic  6.06 us (5%)
  local copies, waits for them, and re-layouts  4.02 us (4%)
    pallas_call x1, Pallas kernels, on_device(): pl.pallas_call(whole, out_shape=(jax.ShapeDtypeStruct((ROWS, C), bf16), j...  102 us
    mul x1, other arithmetic, on_device(): return (feature_grad, weight_sum.astype(f32) * scale[0, 0], gain_grad[:LEV])  6.06 us

profile of v1, /device:TPU:1, one launch (start us, length us, event | category | flops | bytes accessed | tf_op | source)
XLA Modules:
  0.0 113.0 jit_solution(7594384044694865289)
XLA Ops:
  0.6 0.8 copy.10
  1.4 0.6 pad.4
  2.0 102.3 %shard_map.94 = (bf16[1024,256]{1,0:T(8,128)(2,1)}, bf16[7168,256]{1,0:T(8,128)(2,1)}, f32[8,256]{1,0:T(8,128)}, f32[8,128]{1,0:T(8,128)}) custom-call(bf16[1024,256]{1,0:T(8,128)(2,1)} %features_ref.1, bf16[1024,256]{1,0:T(8,128)(2,1)} %grad_ref.1, s32[27,1024]{1,0:T(8,128)} %neighbours_ref.1, s32[32,1,128]{2,1,0:T(1,128)} %bitcast.5, s32[5,1024]{1,0:T(8,128)} %mask_ref.1, ...), custom_call_target="tpu_custom_call" | custom-call | tf_op jit(solution)/shard_map/pallas_call | solution.py:522
  104.3 0.0 copy-start
  104.3 0.0 copy-start.1
  104.3 1.2 %slice.10 = f32[1,1]{1,0:T(1,128)} slice(f32[8,128]{1,0:T(8,128)} %get-tuple-element.9), slice={[0:1], [0:1]} | slice | bytes 8 | tf_op jit(solution)/shard_map/slice | solution.py:575
  105.6 6.1 %convert_multiply_fusion = f32[6912,256]{1,0:T(8,128)} fusion(f32[]{:T(128)} %bitcast.1, bf16[7168,256]{1,0:T(8,128)(2,1)} %get-tuple-element.8), kind=kLoop, calls=%fused_computation | loop fusion | flops 3538944 | bytes 10616836 | tf_op jit(solution)/shard_map/mul | solution.py:575
  111.6 0.0 copy-done
  111.6 0.8 copy.13
  112.4 0.0 copy-done.1
  112.4 0.6 copy.14
Async XLA Ops:
  104.3 7.3 %copy-start = (bf16[1024,256]{1,0:T(8,128)(2,1)S(1)}, bf16[1024,256]{1,0:T(8,128)(2,1)}, u32[]{:S(2)}) copy-start(bf16[1024,256]{1,0:T(8,128)(2,1)} %get-tuple-element.14) | copy-start | bytes 1572868
  104.3 8.1 %copy-start.1 = (f32[8,256]{1,0:T(8,128)S(1)}, f32[8,256]{1,0:T(8,128)}, u32[]{:S(2)}) copy-start(f32[8,256]{1,0:T(8,128)} %get-tuple-element.10) | copy-start | bytes 24580

commit v2 on v1

--- a/solution.py
+++ b/solution.py
@@ -16,14 +16,13 @@
 GHOSTS = PEERS * BUCKET
 SLOTS = ROWS + GHOSTS
 LEV = 5
-T = 4
+T = 2
 NG = 28 // T
 R = T * C
 HALF = R // 2
 QUARTER = HALF // 4
 PIECE = HALF // 16
-AHEAD = 2
-LAST_H = NG - AHEAD
+READY = 8 // T
 STEPS = NG + 7
 f32 = jnp.float32
 bf16 = jnp.bfloat16
@@ -56,6 +55,7 @@
     r3,
     weight,
     total,
+    asked,
     wanted,
     owner_t,
     outgoing,
@@ -122,6 +122,10 @@
     gainf[...] = jnp.zeros_like(gainf)
     gainf[0:LEV, :] = gain_ref[...]
     level_out[0] = jnp.dot(maskf[...].astype(bf16), grad_ref[...], preferred_element_type=f32)
+    square = jnp.concatenate([requests_ref[...], jnp.zeros((128 - BUCKET, PEERS), jnp.int32)], axis=0)
+    lists = square.astype(f32).T.astype(jnp.int32)
+    for peer in range(PEERS):
+        asked[peer] = lists[peer : peer + 1, :]
     wanted[pl.ds(col, 1)] = jnp.zeros((1, 1, 128), jnp.int32)
     own = pl.ds(pl.multiple_of(col * BUCKET, BUCKET), BUCKET)
     ghosts[own, :] = jnp.zeros((BUCKET, C), bf16)
@@ -129,12 +133,13 @@
     wpart[TAPS * C :, :] = jnp.zeros(((NG * T - TAPS) * C, C), f32)
     squares[...] = jnp.zeros_like(squares)
     total[...] = jnp.zeros_like(total)
+    ext_t[:, 0:ROWS] = features_ref[...].T
 
     pl.semaphore_wait(barrier, PEERS - 1 + 1 + 3)
 
     def ask(offset, carry):
         peer = (col + offset) % PEERS
-        push(requests_ref.at[peer], wanted.at[col], halo_send.at[0], halo_recv.at[0], (row, peer))
+        push(asked.at[peer], wanted.at[col], halo_send.at[0], halo_recv.at[0], (row, peer))
         return carry
 
     lax.fori_loop(1, PEERS, ask, 0)
@@ -200,70 +205,62 @@
 
     level_start(0)
 
-    ext_t[:, 0:ROWS] = features_ref[...].T
+    def each_pair(group, body):
+        def pair(number, carry):
+            body(number * 2, 2)
+            return carry
+
+        lax.fori_loop(group * (T // 2), jnp.minimum((group + 1) * (T // 2), TAPS // 2), pair, 0)
+
+        @pl.when(group == NG - 1)
+        def _():
+            body(TAPS - 1, 1)
 
     def spread_taps(group):
-        def one_tap(tap, carry):
-            index = neighbours_ref[pl.ds(tap, 1), :]
-            for first in range(0, SLOTS, 256):
-                places = lax.broadcasted_iota(jnp.int16, (256, ROWS), 0)
-                hit = places == (index - first).astype(jnp.int16)
-                chosen = jnp.where(hit, bf16(1), bf16(0))
-                part = jnp.dot(chosen, grad_ref[...], preferred_element_type=f32)
-                spread[tap, first : first + 256, :] = part.astype(bf16)
+        def body(begin, count):
+            for late in range(count):
+                index = neighbours_ref[pl.ds(begin + late, 1), :]
+                for first in range(0, SLOTS, 256):
+                    places = lax.broadcasted_iota(jnp.int16, (256, ROWS), 0)
+                    hit = places == (index - first).astype(jnp.int16)
+                    chosen = jnp.where(hit, bf16(1), bf16(0))
+                    part = jnp.dot(chosen, grad_ref[...], preferred_element_type=f32)
+                    spread[begin + late, first : first + 256, :] = part.astype(bf16)
+
+        each_pair(group, body)
+
+    def weight_taps(group):
+        def body(begin, count):
+            for late in range(count):
+                tap = begin + late
+                wpart[pl.ds(pl.multiple_of(tap * C, C), C), :] = jnp.dot(
+                    ext_t[...], spread[tap], preferred_element_type=f32
+                )
+
+        each_pair(group, body)
+
+    def give_features():
+        wait_for(wanted.at[0 : PEERS - 1], halo_recv.at[0])
+        lists = jnp.broadcast_to(wanted[...], (PEERS, BUCKET, 128)).reshape(GHOSTS, 128)
+        lanes = lax.broadcasted_iota(jnp.int32, (GHOSTS, 128), 1)
+        places = lax.broadcasted_iota(jnp.int32, (GHOSTS, 128), 0) % BUCKET
+        picked = jnp.where(lanes == places, lists.astype(f32), 0.0)
+        octant = jnp.sum(picked, axis=1, keepdims=True).astype(jnp.int32)
+        octants = lax.broadcasted_iota(jnp.int32, (GHOSTS, ROWS), 1)
+        chosen = jnp.where(octants == octant, 1.0, 0.0).astype(bf16)
+        outgoing[...] = jnp.dot(chosen, features_ref[...], preferred_element_type=f32).astype(bf16)
+
+        def give(offset, carry):
+            peer = (col + offset) % PEERS
+            there = pl.ds(pl.multiple_of(peer * BUCKET, BUCKET), BUCKET)
+            push(outgoing.at[there], ghosts.at[own], halo_send.at[1], halo_recv.at[1], (row, peer))
             return carry
 
-        lax.fori_loop(group * T, jnp.minimum(group * T + T, TAPS), one_tap, 0)
-
-    def weight_taps(group):
-        def one_tap(tap, carry):
-            wpart[pl.ds(pl.multiple_of(tap * C, C), C), :] = jnp.dot(
-                ext_t[...], spread[tap], preferred_element_type=f32
-            )
-            return carry
-
-        lax.fori_loop(group * T, jnp.minimum(group * T + T, TAPS), one_tap, 0)
-
-    def prologue(group, carry):
-        spread_taps(group)
-
-        @pl.when(group == 0)
-        def _():
-            wait_for(wanted.at[0 : PEERS - 1], halo_recv.at[0])
-            lists = jnp.broadcast_to(wanted[...], (PEERS, BUCKET, 128)).reshape(GHOSTS, 128)
-            lanes = lax.broadcasted_iota(jnp.int32, (GHOSTS, 128), 1)
-            places = lax.broadcasted_iota(jnp.int32, (GHOSTS, 128), 0) % BUCKET
-            picked = jnp.where(lanes == places, lists.astype(f32), 0.0)
-            octant = jnp.sum(picked, axis=1, keepdims=True).astype(jnp.int32)
-            octants = lax.broadcasted_iota(jnp.int32, (GHOSTS, ROWS), 1)
-            chosen = jnp.where(octants == octant, 1.0, 0.0).astype(bf16)
-            outgoing[...] = jnp.dot(chosen, features_ref[...], preferred_element_type=f32).astype(
-                bf16
-            )
-
-            def give(offset, carry):
-                peer = (col + offset) % PEERS
-                there = pl.ds(pl.multiple_of(peer * BUCKET, BUCKET), BUCKET)
-                push(
-                    outgoing.at[there],
-                    ghosts.at[own],
-                    halo_send.at[1],
-                    halo_recv.at[1],
-                    (row, peer),
-                )
-                return carry
-
-            lax.fori_loop(1, PEERS, give, 0)
-            owner_t[...] = chosen.T
-
-        return carry
-
-    lax.fori_loop(0, AHEAD, prologue, 0)
-    wait_for(ghosts.at[0 : GHOSTS - BUCKET], halo_recv.at[1])
-    ext_t[:, ROWS:] = ghosts[...].T
+        lax.fori_loop(1, PEERS, give, 0)
+        owner_t[...] = chosen.T
 
     def first_of(group):
-        odd = group % 2
+        odd = (group + group // 4) % 2
         return odd, y + (x - y) * odd, x + (y - x) * odd
 
     def peer_first(odd, other):
@@ -392,47 +389,64 @@
 
     stages = (stage0, stage1, stage2, stage3, stage4, stage5, stage6, stage7)
 
-    def conv_tap(tap, start, size):
-        total[start : start + size, :] += lax.dot_general(
-            spread[tap, start : start + size, :],
-            weight[tap],
-            (((1,), (1,)), ((), ())),
-            preferred_element_type=f32,
-        )
+    def conv_taps(begin, count, start, size):
+        value = total[start : start + size, :]
+        for late in range(count):
+            value = value + lax.dot_general(
+                spread[begin + late, start : start + size, :],
+                weight[begin + late],
+                (((1,), (1,)), ((), ())),
+                preferred_element_type=f32,
+            )
+        total[start : start + size, :] = value
 
     def step(now, carry):
+        @pl.when(now == 1)
+        def _():
+            give_features()
+
+        @pl.when(now == READY)
+        def _():
+            wait_for(ghosts.at[0 : GHOSTS - BUCKET], halo_recv.at[1])
+            ext_t[:, ROWS:] = ghosts[...].T
+
+        @pl.when(now < NG)
+        def _():
+            spread_taps(now)
+
         for late, stage in enumerate(stages):
-            group = now - late
-
-            @pl.when(jnp.logical_and(group >= 0, group < NG))
-            def _(stage=stage, group=group):
+            made = now - late
+            double = jnp.logical_and(made >= READY, made < 2 * READY).astype(jnp.int32)
+            single = jnp.logical_and(made >= 2 * READY, made < NG).astype(jnp.int32)
+            begin = double * 2 * (made - READY) + single * made
+
+            def run(group, carry, stage=stage):
                 stage(group)
+                return carry
+
+            lax.fori_loop(begin, begin + 2 * double + single, run, 0)
 
         for level in range(LEV):
 
-            @pl.when(now == level)
+            @pl.when(now == level + 1)
             def _(level=level):
                 level_end(level)
 
         for stage in range(1, 4):
 
-            @pl.when(now == LEV - 1 + stage)
+            @pl.when(now == LEV + stage)
             def _(stage=stage):
                 gain_stage(stage)
 
-        @pl.when(now < LAST_H)
-        def _():
-            spread_taps(now + AHEAD)
-
-        @pl.when(now == LAST_H)
+        @pl.when(now == NG)
         def _():
             weight_copy.wait()
 
-            def ghost_tap(tap, carry):
-                conv_tap(tap, ROWS, GHOSTS)
+            def ghost_taps(number, carry):
+                conv_taps(number * 3, 3, ROWS, GHOSTS)
                 return carry
 
-            lax.fori_loop(0, TAPS, ghost_tap, 0)
+            lax.fori_loop(0, TAPS // 3, ghost_taps, 0)
             terms[...] = total[ROWS:, :].astype(bf16)
 
             def give_back(offset, carry):
@@ -449,16 +463,16 @@
 
             lax.fori_loop(1, PEERS, give_back, 0)
 
-        @pl.when(now > LAST_H)
+        @pl.when(now > NG)
         def _():
-            def own_tap(tap, carry):
-                conv_tap(tap, 0, ROWS)
+            def own_taps(number, carry):
+                conv_taps(number * 3, 3, 0, ROWS)
                 return carry
 
-            begin = jnp.minimum((now - LAST_H - 1) * 5, TAPS)
-            lax.fori_loop(begin, jnp.minimum(begin + 5, TAPS), own_tap, 0)
-
-        @pl.when(now == LAST_H + 7)
+            begin = jnp.minimum((now - NG - 1) * 2, TAPS // 3)
+            lax.fori_loop(begin, jnp.minimum(begin + 2, TAPS // 3), own_taps, 0)
+
+        @pl.when(now == STEPS - 1)
         def _():
             wait_for(returned.at[0 : GHOSTS - BUCKET], halo_recv.at[2])
             term = pooled[...] * gainf[...]
@@ -491,7 +505,7 @@
     norm2 = jnp.sum(jnp.sum(both, axis=1, keepdims=True), axis=0, keepdims=True) + tiny_eps
     factor = jnp.minimum(1.0, clip_norm / jnp.sqrt(norm2))
     gain_out[...] = gain_total * factor
-    scale_out[...] = jnp.broadcast_to(factor, (8, 128))
+    scale_out[...] = factor
 
     def finish(group, carry):
         wait_for(r0.at[group], send.at[0, group])
@@ -516,7 +530,6 @@
 
 
 def on_device(features, grad_out, conv_weight, pool_gain, neighbours, requests, pool_mask):
-    lists = jnp.pad(requests, ((0, 0), (0, 128 - BUCKET)))[:, None, :]
     vmem = pl.BlockSpec(memory_space=pltpu.VMEM)
     dma = pltpu.SemaphoreType.DMA
     feature_grad, weight_sum, gain_grad, scale = pl.pallas_call(
@@ -525,7 +538,7 @@
             jax.ShapeDtypeStruct((ROWS, C), bf16),
             jax.ShapeDtypeStruct((NG * R, C), bf16),
             jax.ShapeDtypeStruct((8, C), f32),
-            jax.ShapeDtypeStruct((8, 128), f32),
+            jax.ShapeDtypeStruct((1, 1), f32),
         ),
         in_specs=[vmem] * 6 + [pl.BlockSpec(memory_space=pl.ANY)],
         out_specs=(vmem, vmem, vmem, vmem),
@@ -541,6 +554,7 @@
             pltpu.VMEM((NG, 8, PIECE, C), bf16),
             pltpu.VMEM((TAPS, C, C), bf16),
             pltpu.VMEM((SLOTS, C), f32),
+            pltpu.VMEM((PEERS, 1, 128), jnp.int32),
             pltpu.VMEM((PEERS, 1, 128), jnp.int32),
             pltpu.VMEM((ROWS, GHOSTS), bf16),
             pltpu.VMEM((GHOSTS, C), bf16),
@@ -570,7 +584,7 @@
         compiler_params=pltpu.CompilerParams(
             collective_id=0, has_side_effects=True, vmem_limit_bytes=58 * 2**20
         ),
-    )(features, grad_out, neighbours, lists, pool_mask, pool_gain, conv_weight)
+    )(features, grad_out, neighbours, requests.T, pool_mask, pool_gain, conv_weight)
     weight_sum = weight_sum[: TAPS * C].reshape(TAPS, C, C)
     return (feature_grad, weight_sum.astype(f32) * scale[0, 0], gain_grad[:LEV])
 

time: 113 us -> 112 us (level)
  local copies, waits for them, and re-layouts: 4.02 us -> 1.4 us
  Pallas kernels: 102 us -> 104 us
    pallas_call x1, Pallas kernels: 102 us -> 104 us  [on_device(): pl.pallas_call(whole, out_shape=(jax.ShapeDtypeStruct((ROWS, C), bf16), j...]
    slice x1 -> x0, local copies, waits for them, and re-layouts: 1.24 us -> none  [on_device(): return (feature_grad, weight_sum.astype(f32) * scale[0, 0], gain_grad[:LEV])]
where the time goes in v2:
time: 112 us
  Pallas kernels  104 us (93%)
  other arithmetic  6.03 us (5%)
  local copies, waits for them, and re-layouts  1.4 us (1%)
    pallas_call x1, Pallas kernels, on_device(): pl.pallas_call(whole, out_shape=(jax.ShapeDtypeStruct((ROWS, C), bf16), j...  104 us
    mul x1, other arithmetic, on_device(): return (feature_grad, weight_sum.astype(f32) * scale[0, 0], gain_grad[:LEV])  6.03 us

profile of v2, /device:TPU:1, one launch (start us, length us, event | category | flops | bytes accessed | tf_op | source)
XLA Modules:
  0.0 111.7 jit_solution(12409887353392102640)
XLA Ops:
  0.6 103.6 %shard_map.94 = (bf16[1024,256]{1,0:T(8,128)(2,1)}, bf16[7168,256]{1,0:T(8,128)(2,1)}, f32[8,256]{1,0:T(8,128)}, f32[1,1]{1,0:T(1,128)}) custom-call(bf16[1024,256]{1,0:T(8,128)(2,1)} %features_ref.1, bf16[1024,256]{1,0:T(8,128)(2,1)} %grad_ref.1, s32[27,1024]{1,0:T(8,128)} %neighbours_ref.1, s32[16,32]{1,0:T(8,128)} %bitcast.5, s32[5,1024]{1,0:T(8,128)} %mask_ref.1, ...), custom_call_target="tpu_custom_call" | custom-call | tf_op jit(solution)/shard_map/pallas_call | solution.py:535
  104.3 0.0 copy-start
  104.3 0.0 copy-start.1
  104.3 6.0 %convert_multiply_fusion = f32[6912,256]{1,0:T(8,128)} fusion(f32[]{:T(128)} %bitcast.1, bf16[7168,256]{1,0:T(8,128)(2,1)} %get-tuple-element.8), kind=kLoop, calls=%fused_computation | loop fusion | flops 3538944 | bytes 10616836 | tf_op jit(solution)/shard_map/mul | solution.py:589
  110.3 0.0 copy-done
  110.3 0.8 copy.12
  111.1 0.0 copy-done.1
  111.1 0.6 copy.13
Async XLA Ops:
  104.3 6.1 %copy-start = (bf16[1024,256]{1,0:T(8,128)(2,1)S(1)}, bf16[1024,256]{1,0:T(8,128)(2,1)}, u32[]{:S(2)}) copy-start(bf16[1024,256]{1,0:T(8,128)(2,1)} %get-tuple-element.14) | copy-start | bytes 1572868
  104.3 6.8 %copy-start.1 = (f32[8,256]{1,0:T(8,128)S(1)}, f32[8,256]{1,0:T(8,128)}, u32[]{:S(2)}) copy-start(f32[8,256]{1,0:T(8,128)} %get-tuple-element.10) | copy-start | bytes 24580

commit v3 on v2

--- a/solution.py
+++ b/solution.py
@@ -16,13 +16,13 @@
 GHOSTS = PEERS * BUCKET
 SLOTS = ROWS + GHOSTS
 LEV = 5
-T = 2
+T = 4
 NG = 28 // T
 R = T * C
 HALF = R // 2
 QUARTER = HALF // 4
 PIECE = HALF // 16
-READY = 8 // T
+READY = 3
 STEPS = NG + 7
 f32 = jnp.float32
 bf16 = jnp.bfloat16
@@ -41,9 +41,10 @@
     gain_ref,
     weight_hbm,
     fgrad_ref,
-    wsum_ref,
+    wsum_hbm,
     gain_out,
     scale_out,
+    wsum_ref,
     spread,
     ext_t,
     wpart,
@@ -56,11 +57,14 @@
     weight,
     total,
     asked,
+    asked_mid,
     wanted,
     owner_t,
     outgoing,
+    outgoing_mid,
     ghosts,
     terms,
+    terms_mid,
     returned,
     maskf,
     gainf,
@@ -81,6 +85,7 @@
     gain_send,
     gain_recv,
     weight_sem,
+    store_sem,
 ):
     row = lax.axis_index("row")
     col = lax.axis_index("col")
@@ -88,6 +93,17 @@
     core = row % 2
     x = col // 8
     z = col % 8
+    y_others = [(y + offset) % 4 for offset in range(1, 4)]
+    x_others = [(x + offset) % 4 for offset in range(1, 4)]
+    z_others = [(z + offset) % 8 for offset in range(1, 8)]
+    y_rows = [other * 2 + core for other in y_others]
+    x_cols = [other * 8 + z for other in x_others]
+    z_cols = [x * 8 + other for other in z_others]
+    other_core = (y * 2 + 1 - core, col)
+    y_peers = [(there, col) for there in y_rows]
+    x_peers = [(row, there) for there in x_cols]
+    z_peers = [(row, there) for there in z_cols]
+    near = y_peers + x_peers + z_peers + [other_core]
 
     def push(src, dst, send_sem, recv_sem, device):
         pltpu.make_async_remote_copy(
@@ -103,19 +119,8 @@
     weight_copy.start()
 
     barrier = pltpu.get_barrier_semaphore()
-
-    def greet(offset, carry):
-        pl.semaphore_signal(
-            barrier, inc=1, device_id=(row, (col + offset) % PEERS), device_id_type=MESH
-        )
-        return carry
-
-    lax.fori_loop(1, PEERS, greet, 0)
-    pl.semaphore_signal(barrier, inc=1, device_id=(y * 2 + 1 - core, col), device_id_type=MESH)
-    for offset in range(1, 4):
-        pl.semaphore_signal(
-            barrier, inc=1, device_id=((y + offset) % 4 * 2 + core, col), device_id_type=MESH
-        )
+    for device in near:
+        pl.semaphore_signal(barrier, inc=1, device_id=device, device_id_type=MESH)
 
     maskf[...] = jnp.zeros_like(maskf)
     maskf[0:LEV, :] = mask_ref[...].astype(f32)
@@ -125,24 +130,35 @@
     square = jnp.concatenate([requests_ref[...], jnp.zeros((128 - BUCKET, PEERS), jnp.int32)], axis=0)
     lists = square.astype(f32).T.astype(jnp.int32)
     for peer in range(PEERS):
-        asked[peer] = lists[peer : peer + 1, :]
-    wanted[pl.ds(col, 1)] = jnp.zeros((1, 1, 128), jnp.int32)
-    own = pl.ds(pl.multiple_of(col * BUCKET, BUCKET), BUCKET)
-    ghosts[own, :] = jnp.zeros((BUCKET, C), bf16)
-    returned[own, :] = jnp.zeros((BUCKET, C), bf16)
+        asked[peer // 8, peer % 8] = lists[peer : peer + 1, :]
     wpart[TAPS * C :, :] = jnp.zeros(((NG * T - TAPS) * C, C), f32)
     squares[...] = jnp.zeros_like(squares)
     total[...] = jnp.zeros_like(total)
     ext_t[:, 0:ROWS] = features_ref[...].T
 
-    pl.semaphore_wait(barrier, PEERS - 1 + 1 + 3)
-
-    def ask(offset, carry):
-        peer = (col + offset) % PEERS
-        push(asked.at[peer], wanted.at[col], halo_send.at[0], halo_recv.at[0], (row, peer))
-        return carry
-
-    lax.fori_loop(1, PEERS, ask, 0)
+    pl.semaphore_wait(barrier, len(near))
+
+    def leg_x(number, src, mid):
+        for other, device in zip(x_others, x_peers):
+            push(src.at[other], mid.at[x], halo_send.at[number], halo_recv.at[number], device)
+        mid[pl.ds(x, 1)] = src[pl.ds(x, 1)]
+
+    def leg_z(number, mid, dst):
+        wait_for(mid.at[0:3], halo_recv.at[number])
+        for other, device in zip(z_others, z_peers):
+            push(
+                mid.at[:, other],
+                dst.at[:, z],
+                halo_send.at[number + 1],
+                halo_recv.at[number + 1],
+                device,
+            )
+        dst[:, pl.ds(z, 1)] = mid[:, pl.ds(z, 1)]
+
+    def leg_end(number, dst):
+        wait_for(dst.at[:, 0:7], halo_recv.at[number + 1])
+
+    leg_x(0, asked, asked_mid)
 
     level_partner = (
         ((y + 2) % 4 * 2 + core, col),
@@ -180,27 +196,24 @@
         )
         gains0[0] = feature_sums * pooled[...]
         push(
-            gains0.at[0], gains0.at[1], gain_send.at[0], gain_recv.at[0], (y * 2 + 1 - core, col)
+            gains0.at[0], gains0.at[1], gain_send.at[0], gain_recv.at[0], other_core
         )
 
     def gain_stage(stage):
         if stage == 1:
             wait_for(gains0.at[1], gain_recv.at[0])
             gains_y[pl.ds(y, 1)] = (gains0[0] + gains0[1])[None]
-            for offset in range(1, 4):
-                device = ((y + offset) % 4 * 2 + core, col)
+            for device in y_peers:
                 push(gains_y.at[y], gains_y.at[y], gain_send.at[1], gain_recv.at[1], device)
         elif stage == 2:
             wait_for(gains_y.at[0:3], gain_recv.at[1])
             gains_x[pl.ds(x, 1)] = jnp.sum(gains_y[...], axis=0, keepdims=True)
-            for offset in range(1, 4):
-                device = (row, (x + offset) % 4 * 8 + z)
+            for device in x_peers:
                 push(gains_x.at[x], gains_x.at[x], gain_send.at[2], gain_recv.at[2], device)
         else:
             wait_for(gains_x.at[0:3], gain_recv.at[2])
             gains_z[pl.ds(z, 1)] = jnp.sum(gains_x[...], axis=0, keepdims=True)
-            for offset in range(1, 8):
-                device = (row, x * 8 + (z + offset) % 8)
+            for device in z_peers:
                 push(gains_z.at[z], gains_z.at[z], gain_send.at[3], gain_recv.at[3], device)
 
     level_start(0)
@@ -216,7 +229,7 @@
         def _():
             body(TAPS - 1, 1)
 
-    def spread_taps(group):
+    def spread_pair(pair):
         def body(begin, count):
             for late in range(count):
                 index = neighbours_ref[pl.ds(begin + late, 1), :]
@@ -227,7 +240,13 @@
                     part = jnp.dot(chosen, grad_ref[...], preferred_element_type=f32)
                     spread[begin + late, first : first + 256, :] = part.astype(bf16)
 
-        each_pair(group, body)
+        @pl.when(pair < TAPS // 2)
+        def _():
+            body(pair * 2, 2)
+
+        @pl.when(pair == TAPS // 2)
+        def _():
+            body(TAPS - 1, 1)
 
     def weight_taps(group):
         def body(begin, count):
@@ -240,36 +259,28 @@
         each_pair(group, body)
 
     def give_features():
-        wait_for(wanted.at[0 : PEERS - 1], halo_recv.at[0])
-        lists = jnp.broadcast_to(wanted[...], (PEERS, BUCKET, 128)).reshape(GHOSTS, 128)
+        leg_end(0, wanted)
+        lists = jnp.broadcast_to(wanted[...].reshape(PEERS, 1, 128), (PEERS, BUCKET, 128)).reshape(GHOSTS, 128)
         lanes = lax.broadcasted_iota(jnp.int32, (GHOSTS, 128), 1)
         places = lax.broadcasted_iota(jnp.int32, (GHOSTS, 128), 0) % BUCKET
         picked = jnp.where(lanes == places, lists.astype(f32), 0.0)
         octant = jnp.sum(picked, axis=1, keepdims=True).astype(jnp.int32)
         octants = lax.broadcasted_iota(jnp.int32, (GHOSTS, ROWS), 1)
         chosen = jnp.where(octants == octant, 1.0, 0.0).astype(bf16)
-        outgoing[...] = jnp.dot(chosen, features_ref[...], preferred_element_type=f32).astype(bf16)
-
-        def give(offset, carry):
-            peer = (col + offset) % PEERS
-            there = pl.ds(pl.multiple_of(peer * BUCKET, BUCKET), BUCKET)
-            push(outgoing.at[there], ghosts.at[own], halo_send.at[1], halo_recv.at[1], (row, peer))
-            return carry
-
-        lax.fori_loop(1, PEERS, give, 0)
+        taken = jnp.dot(chosen, features_ref[...], preferred_element_type=f32).astype(bf16)
+        outgoing[...] = taken.reshape(4, 8, BUCKET, C)
+        leg_x(2, outgoing, outgoing_mid)
         owner_t[...] = chosen.T
 
-    def first_of(group):
+    def order_of(group):
         odd = (group + group // 4) % 2
         return odd, y + (x - y) * odd, x + (y - x) * odd
 
-    def peer_first(odd, other):
-        return ((other + (y - other) * odd) * 2 + core, (x + (other - x) * odd) * 8 + z)
-
-    def peer_second(odd, other):
-        return ((y + (other - y) * odd) * 2 + core, (other + (x - other) * odd) * 8 + z)
-
-    other_core = (y * 2 + 1 - core, col)
+    def peers_of(odd):
+        chips = [b_ + (a_ - b_) * odd for a_, b_ in zip(x_others, y_others)]
+        rows = [there + (row - there) * odd for there in y_rows]
+        cols = [col + (there - col) * odd for there in x_cols]
+        return zip(chips, zip(rows, cols))
 
     def rows_of(start, size):
         return pl.ds(pl.multiple_of(start, PIECE), size)
@@ -280,90 +291,86 @@
         push(
             wpart.at[rows_of(base + (1 - core) * HALF, HALF)],
             r0.at[group],
-            send.at[0, group],
+            send.at[0],
             recv.at[0, group],
             other_core,
         )
 
     def stage1(group):
-        odd, first, second = first_of(group)
+        odd, first, second = order_of(group)
         wait_for(r0.at[group], recv.at[0, group])
         mine = rows_of(group * R + core * HALF, HALF)
         a1[group] = (wpart[mine, :] + r0[group]).astype(bf16)
-        for offset in range(1, 4):
-            other = (first + offset) % 4
+        for place, (other, device) in enumerate(peers_of(odd)):
             push(
                 a1.at[group, rows_of(other * QUARTER, QUARTER)],
-                r1.at[group, offset - 1],
-                send.at[1, group],
+                r1.at[group, place],
+                send.at[1],
                 recv.at[1, group],
-                peer_first(odd, other),
+                device,
             )
 
     def stage2(group):
-        odd, first, second = first_of(group)
+        odd, first, second = order_of(group)
         wait_for(r1.at[group], recv.at[1, group])
         mine = rows_of(group * R + core * HALF + first * QUARTER, QUARTER)
         kept = wpart[mine, :] + r0[group, rows_of(first * QUARTER, QUARTER), :]
         for offset in range(3):
             kept = kept + r1[group, offset].astype(f32)
         a2[group] = kept.astype(bf16)
-        for offset in range(1, 4):
-            other = (second + offset) % 4
+        for place, (other, device) in enumerate(peers_of(1 - odd)):
             push(
                 a2.at[group, rows_of(other * PIECE, PIECE)],
-                r2.at[group, offset - 1],
-                send.at[2, group],
+                r2.at[group, place],
+                send.at[2],
                 recv.at[2, group],
-                peer_second(odd, other),
+                device,
             )
 
     def stage3(group):
-        odd, first, second = first_of(group)
+        odd, first, second = order_of(group)
         wait_for(r2.at[group], recv.at[2, group])
         kept = a2[group, rows_of(second * PIECE, PIECE), :].astype(f32)
         for offset in range(3):
             kept = kept + r2[group, offset].astype(f32)
         r3[group, pl.ds(z, 1)] = kept.astype(bf16)[None]
-        for offset in range(1, 8):
+        for device in z_peers:
             push(
                 r3.at[group, z],
                 r3.at[group, z],
-                send.at[3, group],
+                send.at[3],
                 recv.at[3, group],
-                (row, x * 8 + (z + offset) % 8),
+                device,
             )
 
     def stage4(group):
-        odd, first, second = first_of(group)
+        odd, first, second = order_of(group)
         wait_for(r3.at[group, 0:7], recv.at[3, group])
         kept = r3[group, 0].astype(f32)
         for place in range(1, 8):
             kept = kept + r3[group, place].astype(f32)
         mine = rows_of(group * R + core * HALF + first * QUARTER + second * PIECE, PIECE)
         wsum_ref[mine, :] = kept.astype(bf16)
-        for offset in range(1, 4):
-            other = (second + offset) % 4
+        for place, (other, device) in enumerate(peers_of(1 - odd)):
             push(
                 wsum_ref.at[mine],
                 wsum_ref.at[mine],
-                send.at[4, group],
+                send.at[4],
                 recv.at[4, group],
-                peer_second(odd, other),
+                device,
             )
 
     def stage5(group):
-        odd, first, second = first_of(group)
+        odd, first, second = order_of(group)
         wait_for(r2.at[group], recv.at[4, group])
         mine = rows_of(group * R + core * HALF + first * QUARTER, QUARTER)
-        for offset in range(1, 4):
-            other = (first + offset) % 4
+        for place, (other, device) in enumerate(peers_of(odd)):
             push(
                 wsum_ref.at[mine],
                 wsum_ref.at[mine],
-                send.at[5, group],
+                send.at[5],
                 recv.at[5, group],
-                peer_first(odd, other),
+                device,
             )
 
     def stage6(group):
@@ -372,7 +379,7 @@
         push(
             wsum_ref.at[mine],
             wsum_ref.at[mine],
-            send.at[6, group],
+            send.at[6],
             recv.at[6, group],
             other_core,
         )
@@ -385,6 +392,8 @@
             squares[...] += jnp.sum((value * value).reshape(8, 8, C), axis=0)
             return carry
 
+        done = rows_of(group * R, R)
+        pltpu.make_async_copy(wsum_ref.at[done], wsum_hbm.at[done], store_sem).start()
         lax.fori_loop(0, R // 64, chunk, 0)
 
     stages = (stage0, stage1, stage2, stage3, stage4, stage5, stage6, stage7)
@@ -405,14 +414,32 @@
         def _():
             give_features()
 
+        @pl.when(now == 2)
+        def _():
+            leg_z(2, outgoing_mid, ghosts)
+
         @pl.when(now == READY)
         def _():
-            wait_for(ghosts.at[0 : GHOSTS - BUCKET], halo_recv.at[1])
-            ext_t[:, ROWS:] = ghosts[...].T
+            leg_end(2, ghosts)
+            ext_t[:, ROWS:] = ghosts[...].reshape(GHOSTS, C).T
 
         @pl.when(now < NG)
         def _():
-            spread_taps(now)
+            spread_pair(now * 2)
+
+        @pl.when(now == 0)
+        def _():
+            leg_z(0, asked_mid, wanted)
+
+        for level in range(LEV):
+
+            @pl.when(now == level)
+            def _(level=level):
+                level_end(level)
+
+        @pl.when(now < NG)
+        def _():
+            spread_pair(now * 2 + 1)
 
         for late, stage in enumerate(stages):
             made = now - late
@@ -426,15 +453,9 @@
 
             lax.fori_loop(begin, begin + 2 * double + single, run, 0)
 
-        for level in range(LEV):
-
-            @pl.when(now == level + 1)
-            def _(level=level):
-                level_end(level)
-
         for stage in range(1, 4):
 
-            @pl.when(now == LEV + stage)
+            @pl.when(now == LEV - 1 + stage)
             def _(stage=stage):
                 gain_stage(stage)
 
@@ -447,21 +468,12 @@
                 return carry
 
             lax.fori_loop(0, TAPS // 3, ghost_taps, 0)
-            terms[...] = total[ROWS:, :].astype(bf16)
-
-            def give_back(offset, carry):
-                peer = (col + offset) % PEERS
-                there = pl.ds(pl.multiple_of(peer * BUCKET, BUCKET), BUCKET)
-                push(
-                    terms.at[there],
-                    returned.at[own],
-                    halo_send.at[2],
-                    halo_recv.at[2],
-                    (row, peer),
-                )
-                return carry
-
-            lax.fori_loop(1, PEERS, give_back, 0)
+            terms[...] = total[ROWS:, :].astype(bf16).reshape(4, 8, BUCKET, C)
+            leg_x(4, terms, terms_mid)
+
+        @pl.when(now == NG + 2)
+        def _():
+            leg_z(4, terms_mid, returned)
 
         @pl.when(now > NG)
         def _():
@@ -472,9 +484,10 @@
             begin = jnp.minimum((now - NG - 1) * 2, TAPS // 3)
             lax.fori_loop(begin, jnp.minimum(begin + 2, TAPS // 3), own_taps, 0)
 
-        @pl.when(now == STEPS - 1)
-        def _():
-            wait_for(returned.at[0 : GHOSTS - BUCKET], halo_recv.at[2])
+        @pl.when(now == STEPS - 2)
+        def _():
+            leg_end(4, returned)
+            back = returned[...].reshape(GHOSTS, C)
             term = pooled[...] * gainf[...]
             high = term.astype(bf16)
             rest = term - high.astype(f32)
@@ -486,7 +499,7 @@
             for first in range(0, ROWS, 256):
                 block = slice(first, first + 256)
                 value = total[block, :] + jnp.dot(
-                    owner_t[block, :], returned[...], preferred_element_type=f32
+                    owner_t[block, :], back, preferred_element_type=f32
                 )
                 value = value + jnp.dot(
                     masks[block, :], parts.astype(bf16), preferred_element_type=f32
@@ -507,20 +520,19 @@
     gain_out[...] = gain_total * factor
     scale_out[...] = factor
 
-    def finish(group, carry):
-        wait_for(r0.at[group], send.at[0, group])
-        wait_for(r1.at[group], send.at[1, group])
-        wait_for(r2.at[group], send.at[2, group])
-        wait_for(r3.at[group, 0:7], send.at[3, group])
-        wait_for(r2.at[group], send.at[4, group])
-        wait_for(r1.at[group], send.at[5, group])
-        wait_for(a1.at[group], send.at[6, group])
-        return carry
-
-    lax.fori_loop(0, NG, finish, 0)
-    wait_for(wanted.at[0 : PEERS - 1], halo_send.at[0])
-    wait_for(ghosts.at[0 : GHOSTS - BUCKET], halo_send.at[1])
-    wait_for(ghosts.at[0 : GHOSTS - BUCKET], halo_send.at[2])
+    wait_for(wsum_ref, store_sem)
+    wait_for(r0, send.at[0])
+    wait_for(r1, send.at[1])
+    wait_for(r2, send.at[2])
+    wait_for(r3.at[:, 0:7], send.at[3])
+    wait_for(r2, send.at[4])
+    wait_for(r1, send.at[5])
+    wait_for(a1, send.at[6])
+    wait_for(asked_mid.at[0:3], halo_send.at[0])
+    wait_for(wanted.at[:, 0:7], halo_send.at[1])
+    for number in (2, 4):
+        wait_for(ghosts.at[0:3], halo_send.at[number])
+        wait_for(ghosts.at[:, 0:7], halo_send.at[number + 1])
     for level in range(LEV):
         wait_for(level_in.at[level], level_send.at[level])
     wait_for(gains0.at[0], gain_send.at[0])
@@ -541,8 +553,9 @@
             jax.ShapeDtypeStruct((1, 1), f32),
         ),
         in_specs=[vmem] * 6 + [pl.BlockSpec(memory_space=pl.ANY)],
-        out_specs=(vmem, vmem, vmem, vmem),
+        out_specs=(vmem, pl.BlockSpec(memory_space=pl.ANY), vmem, vmem),
         scratch_shapes=[
+            pltpu.VMEM((NG * R, C), bf16),
             pltpu.VMEM((TAPS, SLOTS, C), bf16),
             pltpu.VMEM((C, SLOTS), bf16),
             pltpu.VMEM((NG * R, C), f32),
@@ -554,13 +567,16 @@
             pltpu.VMEM((NG, 8, PIECE, C), bf16),
             pltpu.VMEM((TAPS, C, C), bf16),
             pltpu.VMEM((SLOTS, C), f32),
-            pltpu.VMEM((PEERS, 1, 128), jnp.int32),
-            pltpu.VMEM((PEERS, 1, 128), jnp.int32),
+            pltpu.VMEM((4, 8, 1, 128), jnp.int32),
+            pltpu.VMEM((4, 8, 1, 128), jnp.int32),
+            pltpu.VMEM((4, 8, 1, 128), jnp.int32),
             pltpu.VMEM((ROWS, GHOSTS), bf16),
-            pltpu.VMEM((GHOSTS, C), bf16),
-            pltpu.VMEM((GHOSTS, C), bf16),
-            pltpu.VMEM((GHOSTS, C), bf16),
-            pltpu.VMEM((GHOSTS, C), bf16),
+            pltpu.VMEM((4, 8, BUCKET, C), bf16),
+            pltpu.VMEM((4, 8, BUCKET, C), bf16),
+            pltpu.VMEM((4, 8, BUCKET, C), bf16),
+            pltpu.VMEM((4, 8, BUCKET, C), bf16),
+            pltpu.VMEM((4, 8, BUCKET, C), bf16),
+            pltpu.VMEM((4, 8, BUCKET, C), bf16),
             pltpu.VMEM((8, ROWS), f32),
             pltpu.VMEM((8, C), f32),
             pltpu.VMEM((LEV, 8, C), f32),
@@ -571,14 +587,15 @@
             pltpu.VMEM((4, 8, C), f32),
             pltpu.VMEM((8, 8, C), f32),
             pltpu.VMEM((8, C), f32),
+            dma((7,)),
             dma((7, NG)),
-            dma((7, NG)),
-            dma((3,)),
-            dma((3,)),
+            dma((6,)),
+            dma((6,)),
             dma((LEV,)),
             dma((LEV,)),
             dma((4,)),
             dma((4,)),
+            dma,
             dma,
         ],
         compiler_params=pltpu.CompilerParams(

time: 112 us -> 106 us (0.946)
  Pallas kernels: 104 us -> 97.3 us
    pallas_call x1, Pallas kernels: 104 us -> 97.3 us  [on_device(): pl.pallas_call(whole, out_shape=(jax.ShapeDtypeStruct((ROWS, C), bf16), j...]
where the time goes in v3:
time: 106 us; the launch traced here: 105 us
  Pallas kernels  97.3 us (92%)
  other arithmetic  6.03 us (6%)
  local copies, waits for them, and re-layouts  1.4 us (1%)
    pallas_call x1, Pallas kernels, on_device(): pl.pallas_call(whole, out_shape=(jax.ShapeDtypeStruct((ROWS, C), bf16), j...  97.3 us
    mul x1, other arithmetic, on_device(): return (feature_grad, weight_sum.astype(f32) * scale[0, 0], gain_grad[:LEV])  6.03 us

profile of v3, /device:TPU:1, one launch (start us, length us, event | category | flops | bytes accessed | tf_op | source)
XLA Modules:
  0.0 105.4 jit_solution(1317517192793435993)
XLA Ops:
  0.6 97.3 %shard_map.94 = (bf16[1024,256]{1,0:T(8,128)(2,1)}, bf16[7168,256]{1,0:T(8,128)(2,1)}, f32[8,256]{1,0:T(8,128)}, f32[1,1]{1,0:T(1,128)}) custom-call(bf16[1024,256]{1,0:T(8,128)(2,1)} %features_ref.1, bf16[1024,256]{1,0:T(8,128)(2,1)} %grad_ref.1, s32[27,1024]{1,0:T(8,128)} %neighbours_ref.1, s32[16,32]{1,0:T(8,128)} %bitcast.5, s32[5,1024]{1,0:T(8,128)} %mask_ref.1, ...), custom_call_target="tpu_custom_call" | custom-call | tf_op jit(solution)/shard_map/pallas_call | solution.py:547
  98.0 0.0 copy-start
  98.0 0.0 copy-start.1
  98.0 6.0 %convert_multiply_fusion = f32[6912,256]{1,0:T(8,128)} fusion(f32[]{:T(128)} %bitcast.1, bf16[7168,256]{1,0:T(8,128)(2,1)} %get-tuple-element.8), kind=kLoop, calls=%fused_computation | loop fusion | flops 3538944 | bytes 10616836 | tf_op jit(solution)/shard_map/mul | solution.py:606
  104.0 0.0 copy-done
  104.0 0.8 copy.12
  104.8 0.0 copy-done.1
  104.8 0.6 copy.13
Async XLA Ops:
  98.0 6.1 %copy-start = (bf16[1024,256]{1,0:T(8,128)(2,1)S(1)}, bf16[1024,256]{1,0:T(8,128)(2,1)}, u32[]{:S(2)}) copy-start(bf16[1024,256]{1,0:T(8,128)(2,1)} %get-tuple-element.14) | copy-start | bytes 1572868
  98.0 6.8 %copy-start.1 = (f32[8,256]{1,0:T(8,128)S(1)}, f32[8,256]{1,0:T(8,128)}, u32[]{:S(2)}) copy-start(f32[8,256]{1,0:T(8,128)} %get-tuple-element.10) | copy-start | bytes 24580

commit v4 on v3

--- a/solution.py
+++ b/solution.py
@@ -22,7 +22,7 @@
 HALF = R // 2
 QUARTER = HALF // 4
 PIECE = HALF // 16
-READY = 3
+READY = 2
 STEPS = NG + 7
 f32 = jnp.float32
 bf16 = jnp.bfloat16
@@ -57,14 +57,11 @@
     weight,
     total,
     asked,
-    asked_mid,
     wanted,
     owner_t,
     outgoing,
-    outgoing_mid,
     ghosts,
     terms,
-    terms_mid,
     returned,
     maskf,
     gainf,
@@ -103,7 +100,9 @@
     y_peers = [(there, col) for there in y_rows]
     x_peers = [(row, there) for there in x_cols]
     z_peers = [(row, there) for there in z_cols]
-    near = y_peers + x_peers + z_peers + [other_core]
+    across_cols = [there * 8 + other for there in x_others for other in z_others]
+    across = [(row, there) for there in across_cols]
+    near = y_peers + x_peers + z_peers + across + [other_core]
 
     def push(src, dst, send_sem, recv_sem, device):
         pltpu.make_async_remote_copy(
@@ -130,7 +129,7 @@
     square = jnp.concatenate([requests_ref[...], jnp.zeros((128 - BUCKET, PEERS), jnp.int32)], axis=0)
     lists = square.astype(f32).T.astype(jnp.int32)
     for peer in range(PEERS):
-        asked[peer // 8, peer % 8] = lists[peer : peer + 1, :]
+        asked[peer] = lists[peer : peer + 1, :]
     wpart[TAPS * C :, :] = jnp.zeros(((NG * T - TAPS) * C, C), f32)
     squares[...] = jnp.zeros_like(squares)
     total[...] = jnp.zeros_like(total)
@@ -138,27 +137,15 @@
 
     pl.semaphore_wait(barrier, len(near))
 
-    def leg_x(number, src, mid):
-        for other, device in zip(x_others, x_peers):
-            push(src.at[other], mid.at[x], halo_send.at[number], halo_recv.at[number], device)
-        mid[pl.ds(x, 1)] = src[pl.ds(x, 1)]
-
-    def leg_z(number, mid, dst):
-        wait_for(mid.at[0:3], halo_recv.at[number])
-        for other, device in zip(z_others, z_peers):
-            push(
-                mid.at[:, other],
-                dst.at[:, z],
-                halo_send.at[number + 1],
-                halo_recv.at[number + 1],
-                device,
-            )
-        dst[:, pl.ds(z, 1)] = mid[:, pl.ds(z, 1)]
-
-    def leg_end(number, dst):
-        wait_for(dst.at[:, 0:7], halo_recv.at[number + 1])
-
-    leg_x(0, asked, asked_mid)
+    def exchange(number, src, dst):
+        for peer in z_cols + x_cols + across_cols:
+            push(src.at[peer], dst.at[col], halo_send.at[number], halo_recv.at[number], (row, peer))
+        dst[pl.ds(col, 1)] = src[pl.ds(col, 1)]
+
+    def arrived(number, dst, sems):
+        wait_for(dst.at[0 : PEERS - 1], sems.at[number])
+
+    exchange(0, asked, wanted)
 
     level_partner = (
         ((y + 2) % 4 * 2 + core, col),
@@ -259,7 +246,7 @@
         each_pair(group, body)
 
     def give_features():
-        leg_end(0, wanted)
+        arrived(0, wanted, halo_recv)
         lists = jnp.broadcast_to(wanted[...].reshape(PEERS, 1, 128), (PEERS, BUCKET, 128)).reshape(GHOSTS, 128)
         lanes = lax.broadcasted_iota(jnp.int32, (GHOSTS, 128), 1)
         places = lax.broadcasted_iota(jnp.int32, (GHOSTS, 128), 0) % BUCKET
@@ -268,8 +255,8 @@
         octants = lax.broadcasted_iota(jnp.int32, (GHOSTS, ROWS), 1)
         chosen = jnp.where(octants == octant, 1.0, 0.0).astype(bf16)
         taken = jnp.dot(chosen, features_ref[...], preferred_element_type=f32).astype(bf16)
-        outgoing[...] = taken.reshape(4, 8, BUCKET, C)
-        leg_x(2, outgoing, outgoing_mid)
+        outgoing[...] = taken.reshape(PEERS, BUCKET, C)
+        exchange(1, outgoing, ghosts)
         owner_t[...] = chosen.T
 
     def order_of(group):
@@ -410,30 +397,22 @@
         total[start : start + size, :] = value
 
     def step(now, carry):
-        @pl.when(now == 1)
+        @pl.when(now == READY)
+        def _():
+            arrived(1, ghosts, halo_recv)
+            ext_t[:, ROWS:] = ghosts[...].reshape(GHOSTS, C).T
+
+        @pl.when(now < NG)
+        def _():
+            spread_pair(now * 2)
+
+        @pl.when(now == 0)
         def _():
             give_features()
 
-        @pl.when(now == 2)
-        def _():
-            leg_z(2, outgoing_mid, ghosts)
-
-        @pl.when(now == READY)
-        def _():
-            leg_end(2, ghosts)
-            ext_t[:, ROWS:] = ghosts[...].reshape(GHOSTS, C).T
-
-        @pl.when(now < NG)
-        def _():
-            spread_pair(now * 2)
-
-        @pl.when(now == 0)
-        def _():
-            leg_z(0, asked_mid, wanted)
-
         for level in range(LEV):
 
-            @pl.when(now == level)
+            @pl.when(now == level + 1)
             def _(level=level):
                 level_end(level)
 
@@ -455,7 +434,7 @@
 
         for stage in range(1, 4):
 
-            @pl.when(now == LEV - 1 + stage)
+            @pl.when(now == LEV + stage)
             def _(stage=stage):
                 gain_stage(stage)
 
@@ -468,12 +447,8 @@
                 return carry
 
             lax.fori_loop(0, TAPS // 3, ghost_taps, 0)
-            terms[...] = total[ROWS:, :].astype(bf16).reshape(4, 8, BUCKET, C)
-            leg_x(4, terms, terms_mid)
-
-        @pl.when(now == NG + 2)
-        def _():
-            leg_z(4, terms_mid, returned)
+            terms[...] = total[ROWS:, :].astype(bf16).reshape(PEERS, BUCKET, C)
+            exchange(2, terms, returned)
 
         @pl.when(now > NG)
         def _():
@@ -486,7 +461,7 @@
 
         @pl.when(now == STEPS - 2)
         def _():
-            leg_end(4, returned)
+            arrived(2, returned, halo_recv)
             back = returned[...].reshape(GHOSTS, C)
             term = pooled[...] * gainf[...]
             high = term.astype(bf16)
@@ -528,17 +503,26 @@
     wait_for(r2, send.at[4])
     wait_for(r1, send.at[5])
     wait_for(a1, send.at[6])
-    wait_for(asked_mid.at[0:3], halo_send.at[0])
-    wait_for(wanted.at[:, 0:7], halo_send.at[1])
-    for number in (2, 4):
-        wait_for(ghosts.at[0:3], halo_send.at[number])
-        wait_for(ghosts.at[:, 0:7], halo_send.at[number + 1])
+    arrived(0, wanted, halo_send)
+    arrived(1, ghosts, halo_send)
+    arrived(2, returned, halo_send)
     for level in range(LEV):
         wait_for(level_in.at[level], level_send.at[level])
     wait_for(gains0.at[0], gain_send.at[0])
     wait_for(gains_y.at[0:3], gain_send.at[1])
     wait_for(gains_x.at[0:3], gain_send.at[2])
     wait_for(gains_z.at[0:7], gain_send.at[3])
+
+
+def scaled(scale_ref, sum_ref, gain_ref, fgrad_in, out_ref, gain_out, fgrad_out):
+    here = pl.program_id(0)
+
+    @pl.when(here == 0)
+    def _():
+        gain_out[...] = gain_ref[0:LEV, :]
+
+    fgrad_out[...] = fgrad_in[...]
+    out_ref[...] = sum_ref[...].astype(f32) * scale_ref[0, 0]
 
 
 def on_device(features, grad_out, conv_weight, pool_gain, neighbours, requests, pool_mask):
@@ -567,16 +551,13 @@
             pltpu.VMEM((NG, 8, PIECE, C), bf16),
             pltpu.VMEM((TAPS, C, C), bf16),
             pltpu.VMEM((SLOTS, C), f32),
-            pltpu.VMEM((4, 8, 1, 128), jnp.int32),
-            pltpu.VMEM((4, 8, 1, 128), jnp.int32),
-            pltpu.VMEM((4, 8, 1, 128), jnp.int32),
+            pltpu.VMEM((PEERS, 1, 128), jnp.int32),
+            pltpu.VMEM((PEERS, 1, 128), jnp.int32),
             pltpu.VMEM((ROWS, GHOSTS), bf16),
-            pltpu.VMEM((4, 8, BUCKET, C), bf16),
-            pltpu.VMEM((4, 8, BUCKET, C), bf16),
-            pltpu.VMEM((4, 8, BUCKET, C), bf16),
-            pltpu.VMEM((4, 8, BUCKET, C), bf16),
-            pltpu.VMEM((4, 8, BUCKET, C), bf16),
-            pltpu.VMEM((4, 8, BUCKET, C), bf16),
+            pltpu.VMEM((PEERS, BUCKET, C), bf16),
+            pltpu.VMEM((PEERS, BUCKET, C), bf16),
+            pltpu.VMEM((PEERS, BUCKET, C), bf16),
+            pltpu.VMEM((PEERS, BUCKET, C), bf16),
             pltpu.VMEM((8, ROWS), f32),
             pltpu.VMEM((8, C), f32),
             pltpu.VMEM((LEV, 8, C), f32),
@@ -589,8 +570,8 @@
             pltpu.VMEM((8, C), f32),
             dma((7,)),
             dma((7, NG)),
-            dma((6,)),
-            dma((6,)),
+            dma((3,)),
+            dma((3,)),
             dma((LEV,)),
             dma((LEV,)),
             dma((4,)),
@@ -602,8 +583,29 @@
             collective_id=0, has_side_effects=True, vmem_limit_bytes=58 * 2**20
         ),
     )(features, grad_out, neighbours, requests.T, pool_mask, pool_gain, conv_weight)
-    weight_sum = weight_sum[: TAPS * C].reshape(TAPS, C, C)
-    return (feature_grad, weight_sum.astype(f32) * scale[0, 0], gain_grad[:LEV])
+    rows = 9 * C
+    weight_grad, gain_grad, feature_grad = pl.pallas_call(
+        scaled,
+        grid=(TAPS * C // rows,),
+        out_shape=(
+            jax.ShapeDtypeStruct((TAPS * C, C), f32),
+            jax.ShapeDtypeStruct((LEV, C), f32),
+            jax.ShapeDtypeStruct((ROWS, C), bf16),
+        ),
+        in_specs=[
+            pl.BlockSpec(memory_space=pltpu.SMEM),
+            pl.BlockSpec((rows, C), lambda i: (i, 0)),
+            pl.BlockSpec((8, C), lambda i: (0, 0)),
+            pl.BlockSpec((ROWS, C), lambda i: (0, 0)),
+        ],
+        out_specs=(
+            pl.BlockSpec((rows, C), lambda i: (i, 0)),
+            pl.BlockSpec((LEV, C), lambda i: (0, 0)),
+            pl.BlockSpec((ROWS, C), lambda i: (0, 0)),
+        ),
+        compiler_params=pltpu.CompilerParams(vmem_limit_bytes=60 * 2**20),
+    )(scale, weight_sum, gain_grad, feature_grad)
+    return (feature_grad, weight_grad.reshape(TAPS, C, C), gain_grad)
 
 
 def solution(mesh):

time: 106 us -> 102 us (0.962)
  other arithmetic: 6.03 us -> 0 us
  Pallas kernels: 97.3 us -> 101 us
  local copies, waits for them, and re-layouts: 1.4 us -> 0 us
    pallas_call x0 -> x1, Pallas kernels: none -> 6.12 us  [on_device(): pl.pallas_call(scaled, grid=(TAPS * C // rows,), out_shape=(jax.ShapeDtyp...]
    mul x1 -> x0, other arithmetic: 6.03 us -> none  [on_device(): return (feature_grad, weight_sum.astype(f32) * scale[0, 0], gain_grad[:LEV])]
    pallas_call x1, Pallas kernels: 97.3 us -> 95.2 us  [on_device(): pl.pallas_call(whole, out_shape=(jax.ShapeDtypeStruct((ROWS, C), bf16), j...]
    unnamed x6 -> x0, local copies, waits for them, and re-layouts: 1.4 us -> none
where the time goes in v4:
time: 102 us
  Pallas kernels  101 us (99%)
    pallas_call x1, Pallas kernels, on_device(): pl.pallas_call(whole, out_shape=(jax.ShapeDtypeStruct((ROWS, C), bf16), j...  95.2 us
    pallas_call x1, Pallas kernels, on_device(): pl.pallas_call(scaled, grid=(TAPS * C // rows,), out_shape=(jax.ShapeDtyp...  6.12 us

profile of v4, /device:TPU:1, one launch (start us, length us, event | category | flops | bytes accessed | tf_op | source)
XLA Modules:
  0.0 101.9 jit_solution(6816405335955320905)
XLA Ops:
  0.6 95.2 %shard_map.94 = (bf16[1024,256]{1,0:T(8,128)(2,1)}, bf16[7168,256]{1,0:T(8,128)(2,1)}, f32[8,256]{1,0:T(8,128)}, f32[1,1]{1,0:T(1,128)}) custom-call(bf16[1024,256]{1,0:T(8,128)(2,1)} %features_ref.1, bf16[1024,256]{1,0:T(8,128)(2,1)} %grad_ref.1, s32[27,1024]{1,0:T(8,128)} %neighbours_ref.1, s32[16,32]{1,0:T(8,128)} %bitcast.2, s32[5,1024]{1,0:T(8,128)} %mask_ref.1, ...), custom_call_target="tpu_custom_call" | custom-call | tf_op jit(solution)/shard_map/pallas_call | solution.py:531
  95.8 6.1 %shard_map.95 = (f32[6912,256]{1,0:T(8,128)}, f32[5,256]{1,0:T(8,128)}, bf16[1024,256]{1,0:T(8,128)(2,1)}) custom-call(f32[1,1]{1,0:T(1,128)} %get-tuple-element.10.scale_ref, bf16[7168,256]{1,0:T(8,128)(2,1)} %get-tuple-element.11.sum_ref, f32[8,256]{1,0:T(8,128)} %get-tuple-element.12.gain_ref, bf16[1024,256]{1,0:T(8,128)(2,1)} %get-tuple-element.13.fgrad_in), custom_call_target="tpu_custom_call" | custom-call | tf_op jit(solution)/shard_map/pallas_call | solution.py:587

commit v5 on v4

--- a/solution.py
+++ b/solution.py
@@ -58,6 +58,7 @@
     total,
     asked,
     wanted,
+    owner,
     owner_t,
     outgoing,
     ghosts,
@@ -257,7 +258,7 @@
         taken = jnp.dot(chosen, features_ref[...], preferred_element_type=f32).astype(bf16)
         outgoing[...] = taken.reshape(PEERS, BUCKET, C)
         exchange(1, outgoing, ghosts)
-        owner_t[...] = chosen.T
+        owner[...] = chosen
 
     def order_of(group):
         odd = (group + group // 4) % 2
@@ -449,6 +450,10 @@
             lax.fori_loop(0, TAPS // 3, ghost_taps, 0)
             terms[...] = total[ROWS:, :].astype(bf16).reshape(PEERS, BUCKET, C)
             exchange(2, terms, returned)
+
+        @pl.when(now == NG + 3)
+        def _():
+            owner_t[...] = owner[...].T
 
         @pl.when(now > NG)
         def _():
@@ -553,6 +558,7 @@
             pltpu.VMEM((SLOTS, C), f32),
             pltpu.VMEM((PEERS, 1, 128), jnp.int32),
             pltpu.VMEM((PEERS, 1, 128), jnp.int32),
+            pltpu.VMEM((GHOSTS, ROWS), bf16),
             pltpu.VMEM((ROWS, GHOSTS), bf16),
             pltpu.VMEM((PEERS, BUCKET, C), bf16),
             pltpu.VMEM((PEERS, BUCKET, C), bf16),

time: 102 us -> 102 us (level)
  no operation moved by 1% of the time
where the time goes in v5:
time: 102 us
  Pallas kernels  102 us (100%)
    pallas_call x1, Pallas kernels, on_device(): pl.pallas_call(whole, out_shape=(jax.ShapeDtypeStruct((ROWS, C), bf16), j...  95.4 us
    pallas_call x1, Pallas kernels, on_device(): pl.pallas_call(scaled, grid=(TAPS * C // rows,), out_shape=(jax.ShapeDtyp...  6.12 us

profile of v5, /device:TPU:1, one launch (start us, length us, event | category | flops | bytes accessed | tf_op | source)
XLA Modules:
  0.0 102.2 jit_solution(8447161889464197345)
XLA Ops:
  0.6 95.4 %shard_map.94 = (bf16[1024,256]{1,0:T(8,128)(2,1)}, bf16[7168,256]{1,0:T(8,128)(2,1)}, f32[8,256]{1,0:T(8,128)}, f32[1,1]{1,0:T(1,128)}) custom-call(bf16[1024,256]{1,0:T(8,128)(2,1)} %features_ref.1, bf16[1024,256]{1,0:T(8,128)(2,1)} %grad_ref.1, s32[27,1024]{1,0:T(8,128)} %neighbours_ref.1, s32[16,32]{1,0:T(8,128)} %bitcast.2, s32[5,1024]{1,0:T(8,128)} %mask_ref.1, ...), custom_call_target="tpu_custom_call" | custom-call | tf_op jit(solution)/shard_map/pallas_call | solution.py:536
  96.0 6.1 %shard_map.95 = (f32[6912,256]{1,0:T(8,128)}, f32[5,256]{1,0:T(8,128)}, bf16[1024,256]{1,0:T(8,128)(2,1)}) custom-call(f32[1,1]{1,0:T(1,128)} %get-tuple-element.10.scale_ref, bf16[7168,256]{1,0:T(8,128)(2,1)} %get-tuple-element.11.sum_ref, f32[8,256]{1,0:T(8,128)} %get-tuple-element.12.gain_ref, bf16[1024,256]{1,0:T(8,128)(2,1)} %get-tuple-element.13.fgrad_in), custom_call_target="tpu_custom_call" | custom-call | tf_op jit(solution)/shard_map/pallas_call | solution.py:593
